TPU v7x, 256 devices: a whole 4x4x8 slice. The times are simulated.
256 devices in a mesh: wide: 32 (over z_hi, y, core), narrow: 8 (over x, z_lo).
Axes of the slice: x: 4, y: 4, z: 8 (z_hi: 4, z_lo: 2; z = z_hi * 2 + z_lo), core: 2. Of those that a mesh axis runs over, the one named last changes fastest.
Arguments:
- proj_a: bfloat16 [256, 32, 1024], P('narrow', None, 'wide'), may hold values from -12 to 12
- proj_b: bfloat16 [256, 32, 1024], P('wide', None, 'narrow'), may hold values from -12 to 12
- out_weight: bfloat16 [1024, 128], replicated, may hold values from -0.75 to 0.75
- out_bias: float32 [128], replicated, may hold values from -3 to 3
- pair_cotangent: bfloat16 [1024, 1024, 128], P('wide', 'narrow'), may hold values from -6 to 6
Outputs:
- pair_update: bfloat16 [1024, 1024, 128], P('wide', 'narrow')
- grad_a: bfloat16 [256, 32, 1024], P('narrow', None, 'wide')
- grad_b: bfloat16 [256, 32, 1024], P('wide', None, 'narrow')
All inputs are finite; a program needn't handle non-finite values.
Results may differ from a plain program's by a relative error of at most 0.0049.
Values may be sent and summed in bfloat16 or wider, within the bound.
No kernel may reach another device: no remote copies, remote signals or barrier semaphores. Data moves between devices by JAX's collectives and lax.ppermute only.
A program may use at most 128 MiB of HBM per device.

v0:
```python
import jax
import jax.numpy as jnp
from jax import lax
from jax.sharding import PartitionSpec as P


def reduce_for_a(grad_outer, b_full):
    a_terms = jnp.einsum("ijce,sej->sci", grad_outer, b_full, preferred_element_type=jnp.float32)
    return lax.psum_scatter(a_terms, "narrow", scatter_dimension=0, tiled=True)


def reduce_for_b(grad_outer, a_full):
    b_partial = jnp.einsum("ijce,sci->sej", grad_outer, a_full, preferred_element_type=jnp.float32)
    return lax.psum_scatter(b_partial, "wide", scatter_dimension=0, tiled=True)


def shards(proj_a, proj_b, out_weight, out_bias, pair_cotangent):
    a_full = lax.all_gather(proj_a, "narrow", axis=0, tiled=True)
    b_full = lax.all_gather(proj_b, "wide", axis=0, tiled=True)
    seqs = a_full.shape[0]
    chans = a_full.shape[1]
    rows = a_full.shape[2]
    cols = proj_b.shape[2]
    scale = 1.0 / seqs
    summed = jnp.einsum("sci,sej->ijce", a_full, b_full, preferred_element_type=jnp.float32)
    outer = (summed * scale).astype(jnp.bfloat16).reshape(rows, cols, chans * chans)
    update = jnp.einsum("ijf,fk->ijk", outer, out_weight, preferred_element_type=jnp.float32)
    pair_update = (update + out_bias).astype(jnp.bfloat16)
    grad_outer = jnp.einsum(
        "ijk,fk->ijf", pair_cotangent, out_weight, preferred_element_type=jnp.float32
    )
    grad_outer = grad_outer.astype(jnp.bfloat16).reshape(rows, cols, chans, chans)
    a_summed = reduce_for_a(grad_outer, b_full)
    b_summed = reduce_for_b(grad_outer, a_full)
    grad_a = (a_summed * scale).astype(jnp.bfloat16)
    grad_b = (b_summed * scale).astype(jnp.bfloat16)
    return (pair_update, grad_a, grad_b)


def solution(mesh):
    placed = (
        P("narrow", None, "wide"),
        P("wide", None, "narrow"),
        P(),
        P(),
        P("wide", "narrow", None),
    )
    return jax.shard_map(
        shards,
        mesh=mesh,
        in_specs=placed,
        out_specs=(P("wide", "narrow", None), P("narrow", None, "wide"), P("wide", None, "narrow")),
        check_vma=False,
    )
```

profile of v0, /device:TPU:1, one launch (start us, length us, event | category | flops | bytes accessed | tf_op | source)
XLA Modules:
  0.0 275.7 jit_solution(8928491309425554105)
XLA Ops:
  7.2 0.0 all-gather.2.cloned.1.call-start
  7.2 1.6 copy.25
  8.8 0.0 all-gather.2.cloned.1.call-update
  8.8 0.0 reduce-scatter.7.cloned.1.call-start
  8.9 6.5 %convolution_convert_fusion = bf16[32,128,1024]{2,1,0:T(8,128)(2,1)} fusion(bf16[32,128,128]{2,1,0:T(8,128)(2,1)S(1)} %copy-done, bf16[1024,128]{1,0:T(8,128)(2,1)} %param.7), kind=kOutput, calls=%fused_computation.5 | convolution fusion | flops 1077936128 | bytes 9699328 | tf_op jit(solution)/shard_map/ijk,fk->ijf/dot_general | solution.py:29
  15.4 11.9 %copy.29 = bf16[32,128,1024]{1,2,0:T(8,128)(2,1)} copy(bf16[32,128,1024]{2,1,0:T(8,128)(2,1)} %convolution_convert_fusion) | data formatting | bytes 16777216 | tf_op jit(solution)/shard_map/convert_element_type | solution.py:32
  27.4 43.9 %all-gather.2.cloned.1.call-done = bf16[256,32,128]{2,0,1:T(8,128)(2,1)} async-done(((bf16[8,32,128]{2,0,1:T(8,128)(2,1)}), bf16[256,32,128]{2,0,1:T(8,128)(2,1)}) %all-gather.2.cloned.1.call-update) | async-done | bytes 2097168 | tf_op jit(solution)/shard_map/all_gather | solution.py:19
  71.3 6.5 %fusion.12 = f32[256,32,32]{0,1,2:T(8,128)S(1)} fusion(bf16[256,32,128]{2,0,1:T(8,128)(2,1)} %all-gather.2.cloned.1.call-done, bf16[32,128,32,32]{1,3,2,0:T(8,128)(2,1)} %bitcast.40), kind=kOutput, calls=%fused_computation.13 | convolution fusion | flops 2147483648 | bytes 11534336 | tf_op jit(solution)/shard_map/ijce,sej->sci/dot_general | solution.py:8
  77.8 4.4 %copy.39 = f32[256,32,32]{1,2,0:T(8,128)} copy(f32[256,32,32]{0,1,2:T(8,128)S(1)} %fusion.12) | data formatting | bytes 2097152
  82.2 4.6 %reshape.21 = f32[256,1024]{1,0:T(8,128)} reshape(f32[256,32,32]{2,1,0:T(8,128)} %bitcast.39) | data formatting | bytes 2097152
  86.8 0.0 reduce-scatter.5.cloned.1.call-start
  86.9 63.2 %all_gather.7 = bf16[256,32,32]{2,1,0:T(8,128)(2,1)S(1)} all-gather(bf16[32,32,32]{2,1,0:T(8,128)(2,1)S(1)} %copy-done.1), channel_id=1, replica_groups=mesh['wide'=32,'narrow'=8] {'narrow'}, dimensions={0}, use_global_device_ids=true | all-gather | bytes 589824 | tf_op jit(solution)/shard_map/all_gather | solution.py:18
  150.1 16.9 %fusion.5 = f32[256,32,128]{0,2,1:T(8,128)} fusion(bf16[32,128,32,32]{1,3,2,0:T(8,128)(2,1)} %bitcast.41, bf16[256,32,32]{2,1,0:T(8,128)(2,1)S(1)} %all_gather.7), kind=kOutput, calls=%fused_computation.7 | convolution fusion | flops 2147483648 | bytes 13107200 | tf_op jit(solution)/shard_map/ijce,sci->sej/dot_general | solution.py:13
  167.0 5.5 %copy.33 = f32[256,32,128]{2,1,0:T(8,128)} copy(f32[256,32,128]{0,2,1:T(8,128)} %fusion.5) | data formatting | bytes 8388608 | tf_op jit(solution)/shard_map/ijce,sci->sej/transpose | solution.py:13
  172.5 2.4 copy.26
  174.8 7.3 %fusion.4 = bf16[32,128,32,32]{1,0,2,3:T(8,128)(2,1)} fusion(bf16[256,32,128]{2,0,1:T(8,128)(2,1)} %all-gather.2.cloned.1.call-done, bf16[256,32,32]{0,2,1:T(8,128)(2,1)} %copy.26), kind=kOutput, calls=%fused_computation.6 | convolution fusion | flops 2155872256 | bytes 11010048 | tf_op jit(solution)/shard_map/sci,sej->ijce/dot_general | solution.py:25
  182.1 12.3 %copy.27 = bf16[32,128,32,32]{1,3,2,0:T(8,128)(2,1)} copy(bf16[32,128,32,32]{1,0,2,3:T(8,128)(2,1)} %fusion.4) | data formatting | bytes 16777216 | tf_op jit(solution)/shard_map/convert_element_type | solution.py:26
  194.4 7.0 %add_convert_fusion = bf16[32,128,128]{2,1,0:T(8,128)(2,1)} fusion(bf16[32,128,1024]{1,2,0:T(8,128)(2,1)} %bitcast.42, f32[128]{0:T(128)S(1)} %copy-done.3, bf16[1024,128]{1,0:T(8,128)(2,1)S(1)} %copy-done.2), kind=kOutput, calls=%fused_computation.12 | convolution fusion | flops 1074790400 | bytes 9699840 | tf_op jit(solution)/shard_map/ijf,fk->ijk/dot_general | solution.py:27
  201.4 1.1 reshape.22
  202.5 0.3 copy.40
  202.8 0.1 multiply_convert_fusion.1
  202.8 1.2 copy.34
  204.1 63.6 %reduce-scatter.5.cloned.1.call-done = f32[8,32,128]{2,1,0:T(8,128)} async-done(((f32[256,32,128]{2,1,0:T(8,128)}), f32[8,32,128]{2,1,0:T(8,128)}) %reduce-scatter.5.cloned.1.call-update) | async-done | bytes 131088 | tf_op jit(solution)/shard_map/reduce_scatter | solution.py:14
  267.7 1.5 multiply_convert_fusion.2
  (11 shorter events, 0.1 us)
Async XLA Ops:
  7.2 1.7 copy-start
  7.2 64.1 %all-gather.2.cloned.1.call-start = ((), (), s32[]{:S(2)}) async-start(), calls=%async_computation.2 | async-start | bytes 2162688 | tf_op jit(solution)/shard_map/all_gather | solution.py:19
  8.8 192.5 %reduce-scatter.7.cloned.1.call-start = ((), (), s32[]{:S(2)}) async-start(), calls=%async_computation.4 | async-start | bytes 1179648
  77.8 9.1 %copy-start.1 = (bf16[32,32,32]{2,1,0:T(8,128)(2,1)S(1)}, bf16[32,32,32]{2,1,0:T(8,128)(2,1)}, u32[]{:S(2)}) copy-start(bf16[32,32,32]{2,1,0:T(8,128)(2,1)} %param.5) | copy-start | bytes 196612
  86.8 180.9 %reduce-scatter.5.cloned.1.call-start = ((), (), s32[]{:S(2)}) async-start(), calls=%async_computation.3 | async-start | bytes 4325376 | tf_op jit(solution)/shard_map/reduce_scatter | solution.py:14
  182.1 12.3 %copy-start.2 = (bf16[1024,128]{1,0:T(8,128)(2,1)S(1)}, bf16[1024,128]{1,0:T(8,128)(2,1)}, u32[]{:S(2)}) copy-start(bf16[1024,128]{1,0:T(8,128)(2,1)} %param.7) | copy-start | bytes 786436
  182.1 12.3 %copy-start.3 = (f32[128]{0:T(128)S(1)}, f32[128]{0:T(128)}, u32[]{:S(2)}) copy-start(f32[128]{0:T(128)} %param.8) | copy-start | bytes 1540
Sparse Core Ops, SparseCore 0:
  11.1 60.1 all-gather.1
  86.9 52.0 reduce-scatter.6
  172.6 95.0 reduce-scatter.4
where the time goes:
time: 277 us; the launch traced here: 276 us
  waiting for transfers between devices  108 us (39%)
  blocking collectives  63.2 us (23%)
  local copies, waits for them, and re-layouts  45.3 us (16%)
  matrix products  44.2 us (16%)
  between operations  13.8 us (5%)
    reduce_scatter x1, waiting for transfers between devices, reduce_for_b(): return lax.psum_scatter(b_partial, 'wide', scatter_dimension=0, tiled=True)  63.6 us
    all_gather x1, blocking collectives, shards(): a_full = lax.all_gather(proj_a, 'narrow', axis=0, tiled=True)  63.2 us
    all_gather x1, waiting for transfers between devices, shards(): b_full = lax.all_gather(proj_b, 'wide', axis=0, tiled=True)  43.9 us
    dot_general x1, matrix products, reduce_for_b(): jnp.einsum('ijce,sci->sej', grad_outer, a_full, preferred_element_type=jn...  16.9 us
    unnamed x14, local copies, waits for them, and re-layouts  13.2 us
    convert_element_type x1, local copies, waits for them, and re-layouts, shards(): (summed * scale).astype(jnp.bfloat16).reshape(rows, cols, chans * chans)  12.3 us
    convert_element_type x1, local copies, waits for them, and re-layouts, shards(): grad_outer.astype(jnp.bfloat16).reshape(rows, cols, chans, chans)  11.9 us
    dot_general x1, matrix products, shards(): jnp.einsum('sci,sej->ijce', a_full, b_full, preferred_element_type=jnp.fl...  7.26 us
  transfers between devices with their start and end apart: 3, of which 2 were waited for; matrix products, arithmetic and copies ran while one was open for 26% of the time, Pallas kernels for 0%

commit v1 on v0

v1 whole, which is shorter than its diff:
```python
import functools

import jax
import jax.numpy as jnp
from jax import lax
from jax.experimental import pallas as pl
from jax.experimental.pallas import tpu as pltpu
from jax.sharding import PartitionSpec as P

F32 = jnp.float32
BF16 = jnp.bfloat16
C = 32
K = 128
SEQ = 256
ROWS = 32
COLS = 128
SCALE = 1.0 / SEQ
MIB = 1024 * 1024


def wide_perm(dz, dy, dc):
    perm = []
    for w in range(32):
        z, y, c = w // 8, (w // 2) % 4, w % 2
        perm.append((w, (((z + dz) % 4) * 4 + (y + dy) % 4) * 2 + (c ^ dc)))
    return perm


def narrow_perm(dx, dl):
    return [(n, ((n // 2 + dx) % 4) * 2 + ((n % 2) ^ dl)) for n in range(8)]


def send_z(v, k):
    return lax.ppermute(v, "wide", wide_perm(k, 0, 0))


def send_y(v, k):
    return lax.ppermute(v, "wide", wide_perm(0, k, 0))


def send_core(v):
    return lax.ppermute(v, "wide", wide_perm(0, 0, 1))


def send_x(v, k):
    return lax.ppermute(v, "narrow", narrow_perm(k, 0))


def send_l(v):
    return lax.ppermute(v, "narrow", narrow_perm(0, 1))


def own_row(place, rx, rl, yl, core):
    z, y, c, x, l = (place[q] for q in range(5))
    zz = lax.rem(x + rx - z + 8, 4)
    yy = lax.rem(2 * lax.rem(l + rl, 2) + yl - y + 8, 4)
    cc = lax.rem(core + c, 2)
    return pl.multiple_of(((cc * 4 + yy) * 4 + zz) * 8, 8)


def grad_outer_kernel(cot, w, g):
    count = cot.shape[0]
    both = cot[...].reshape(count * COLS, K)
    r = lax.dot_general(w[...], both, (((1,), (1,)), ((), ())), preferred_element_type=F32)
    r = r.astype(BF16)
    for i in range(count):
        for e in range(C):
            g[i * C:(i + 1) * C, e * COLS:(e + 1) * COLS] = r[e * C:(e + 1) * C, i * COLS:(i + 1) * COLS]


def grad_outer(cot, w):
    step = 4
    return pl.pallas_call(
        grad_outer_kernel,
        grid=(ROWS // step,),
        in_specs=[
            pl.BlockSpec((step, COLS, K), lambda r: (r, 0, 0)),
            pl.BlockSpec((C * C, K), lambda r: (0, 0)),
        ],
        out_specs=pl.BlockSpec((step * C, C * COLS), lambda r: (r, 0)),
        out_shape=jax.ShapeDtypeStruct((ROWS * C, C * COLS), BF16),
        compiler_params=pltpu.CompilerParams(vmem_limit_bytes=24 * MIB),
        cost_estimate=pl.CostEstimate(flops=2 * 4096 * 1024 * 128, bytes_accessed=9 * MIB, transcendentals=0),
        name="grad_outer",
    )(cot, w)


def grad_b_kernel(place, x0, x1, x2, x3, g, keep, away, at, order, a):
    @pl.when(pl.program_id(0) == 0)
    def _():
        for rx, piece in enumerate((x0, x1, x2, x3)):
            v = piece[...].astype(F32)
            for rl in range(2):
                for yl in range(2):
                    for core in range(2):
                        at_row = ((rl * 2 + yl) * 2 + core) * 8
                        order[pl.ds(own_row(place, rx, rl, yl, core), 8), :] = v[at_row:at_row + 8, :]
        v = order[...]
        a[...] = v.astype(BF16)
        at[...] = v.T.astype(BF16)

    r = jnp.dot(a[...], g[...], preferred_element_type=F32)
    keep[...] = r[:SEQ // 2]
    away[...] = r[SEQ // 2:].astype(BF16)


def grad_b_terms(place, xs, g):
    step = 512
    half = SEQ // 2
    piece = pl.BlockSpec((64, ROWS * C), lambda r: (0, 0))
    return pl.pallas_call(
        grad_b_kernel,
        grid=(C * COLS // step,),
        in_specs=[pl.BlockSpec(memory_space=pltpu.SMEM)] + [piece] * 4
        + [pl.BlockSpec((ROWS * C, step), lambda r: (0, r))],
        out_specs=[
            pl.BlockSpec((half, step), lambda r: (0, r)),
            pl.BlockSpec((half, step), lambda r: (0, r)),
            pl.BlockSpec((ROWS * C, SEQ), lambda r: (0, 0)),
        ],
        out_shape=[
            jax.ShapeDtypeStruct((half, C * COLS), F32),
            jax.ShapeDtypeStruct((half, C * COLS), BF16),
            jax.ShapeDtypeStruct((ROWS * C, SEQ), BF16),
        ],
        scratch_shapes=[pltpu.VMEM((SEQ, ROWS * C), F32), pltpu.VMEM((SEQ, ROWS * C), BF16)],
        compiler_params=pltpu.CompilerParams(vmem_limit_bytes=24 * MIB),
        cost_estimate=pl.CostEstimate(flops=2 * 4096 * 1024 * 256, bytes_accessed=12 * MIB, transcendentals=0),
        name="grad_b_terms",
    )(place, *xs, g)


def grad_a_kernel(place, b0, b1, b2, b3, b4, b5, b6, b7, g, keep, o1, o2, o3, b, r):
    @pl.when(pl.program_id(0) == 0)
    def _():
        for q, piece in enumerate((b0, b1, b2, b3, b4, b5, b6, b7)):
            b[q * 32:(q + 1) * 32, :] = piece[...]

    r[...] = lax.dot_general(b[...], g[...], (((1,), (1,)), ((), ())), preferred_element_type=F32)
    for rx, out in enumerate((keep, o1, o2, o3)):
        for rl in range(2):
            for yl in range(2):
                both = [r[pl.ds(own_row(place, rx, rl, yl, core), 8), :] for core in range(2)]
                row = (rl * 2 + yl) * 16
                out[row:row + 16, :] = jnp.concatenate(both, 0).astype(out.dtype)


def grad_a_terms(place, bs, g):
    step = 256
    piece = pl.BlockSpec((32, C * COLS), lambda r: (0, 0))
    out = pl.BlockSpec((64, step), lambda r: (0, r))
    return pl.pallas_call(
        grad_a_kernel,
        grid=(ROWS * C // step,),
        in_specs=[pl.BlockSpec(memory_space=pltpu.SMEM)] + [piece] * 8
        + [pl.BlockSpec((step, C * COLS), lambda r: (r, 0))],
        out_specs=[out] * 4,
        out_shape=[jax.ShapeDtypeStruct((64, ROWS * C), F32)]
        + [jax.ShapeDtypeStruct((64, ROWS * C), BF16)] * 3,
        scratch_shapes=[pltpu.VMEM((SEQ, C * COLS), BF16), pltpu.VMEM((SEQ, step), F32)],
        compiler_params=pltpu.CompilerParams(vmem_limit_bytes=24 * MIB),
        cost_estimate=pl.CostEstimate(flops=2 * 4096 * 1024 * 256, bytes_accessed=12 * MIB, transcendentals=0),
        name="grad_a_terms",
    )(place, *bs, g)


def update_kernel(at, b0, b1, b2, b3, b4, b5, b6, b7, wt, bias, out, b, o):
    @pl.when(pl.program_id(0) == 0)
    def _():
        for q, piece in enumerate((b0, b1, b2, b3, b4, b5, b6, b7)):
            b[q * 32:(q + 1) * 32, :] = piece[...]

    count = out.shape[0]
    wide = 8
    for start in range(0, C, wide):
        r = jnp.dot(at[...], b[:, start * COLS:(start + wide) * COLS], preferred_element_type=F32)
        r = (r * SCALE).astype(BF16)
        for i in range(count):
            for e in range(wide):
                row = (start + e) * C
                o[row:row + C, i * COLS:(i + 1) * COLS] = r[i * C:(i + 1) * C, e * COLS:(e + 1) * COLS]
    u = jnp.dot(wt[...], o[...], preferred_element_type=F32)
    for i in range(count):
        out[i] = (u[:, i * COLS:(i + 1) * COLS].T + bias[...]).astype(BF16)


def pair_update(at, bs, wt, bias):
    step = 8
    piece = pl.BlockSpec((32, C * COLS), lambda r: (0, 0))
    return pl.pallas_call(
        update_kernel,
        grid=(ROWS // step,),
        in_specs=[pl.BlockSpec((step * C, SEQ), lambda r: (r, 0))] + [piece] * 8
        + [pl.BlockSpec((K, C * C), lambda r: (0, 0)), pl.BlockSpec((1, K), lambda r: (0, 0))],
        out_specs=pl.BlockSpec((step, COLS, K), lambda r: (r, 0, 0)),
        out_shape=jax.ShapeDtypeStruct((ROWS, COLS, K), BF16),
        scratch_shapes=[pltpu.VMEM((SEQ, C * COLS), BF16), pltpu.VMEM((C * C, step * COLS), BF16)],
        compiler_params=pltpu.CompilerParams(vmem_limit_bytes=24 * MIB),
        cost_estimate=pl.CostEstimate(flops=3 * 4096 * 1024 * 256, bytes_accessed=4 * MIB, transcendentals=0),
        name="pair_update",
    )(at, *bs, wt, bias)


def shards(proj_a, proj_b, out_weight, out_bias, pair_cotangent):
    w = lax.axis_index("wide")
    n = lax.axis_index("narrow")
    place = jnp.stack([w // 8, (w // 2) % 4, w % 2, n // 2, n % 2]).astype(jnp.int32)

    a0 = proj_a.transpose(0, 2, 1).reshape(32, ROWS * C)
    a1 = send_l(a0)
    xs = [jnp.concatenate([a0, a1], 0)]
    xs += [send_x(xs[0], -k) for k in (1, 2, 3)]

    b0 = proj_b.reshape(8, C * COLS)
    zs = jnp.concatenate([b0] + [send_z(b0, -k) for k in (1, 2, 3)], 0)
    ys = [zs] + [send_y(zs, -k) for k in (1, 2, 3)]
    bs = ys + [send_core(v) for v in ys]

    weight = out_weight.reshape(C, C, K).transpose(1, 0, 2).reshape(C * C, K)
    g = grad_outer(pair_cotangent, weight)

    keep, away, at = grad_b_terms(place, xs, g)
    parts = {}
    for k in (2, 1, 3, 0):
        part = slice(32 * k, 32 * (k + 1))
        parts[k] = keep[part] + send_core(away[part]).astype(F32)
    total = parts[0]
    for k in (2, 1, 3):
        total = total + send_y(parts[k].astype(BF16), k).astype(F32)
    b_summed = total[:8]
    for k in (1, 2, 3):
        b_summed = b_summed + send_z(total[8 * k:8 * (k + 1)].astype(BF16), k).astype(F32)
    grad_b = (b_summed * SCALE).astype(BF16).reshape(8, C, COLS)

    kept, *others = grad_a_terms(place, bs, g)
    for k in (1, 2, 3):
        kept = kept + send_x(others[k - 1], k).astype(F32)
    a_summed = kept[:32] + send_l(kept[32:].astype(BF16)).astype(F32)
    grad_a = (a_summed * SCALE).astype(BF16).reshape(32, ROWS, C).transpose(0, 2, 1)

    update = pair_update(at, bs, weight.T, out_bias.reshape(1, K))
    return (update, grad_a, grad_b)


def solution(mesh):
    placed = (
        P("narrow", None, "wide"),
        P("wide", None, "narrow"),
        P(),
        P(),
        P("wide", "narrow", None),
    )
    return jax.shard_map(
        shards,
        mesh=mesh,
        in_specs=placed,
        out_specs=(P("wide", "narrow", None), P("narrow", None, "wide"), P("wide", None, "narrow")),
        check_vma=False,
    )
```

time: 277 us -> 86.3 us (0.31)
  waiting for transfers between devices: 108 us -> 6.61 us
  blocking collectives: 63.2 us -> 0 us
  matrix products: 44.2 us -> 0 us
  starting transfers between devices: 0.12 us -> 41 us
  local copies, waits for them, and re-layouts: 45.3 us -> 13.9 us
  Pallas kernels: 0 us -> 21 us
  between operations: 13.8 us -> 0.93 us
    reduce_scatter x1 -> x0, waiting for transfers between devices: 63.6 us -> none  [reduce_for_b(): return lax.psum_scatter(b_partial, 'wide', scatter_dimension=0, tiled=True)]
    all_gather x1 -> x0, blocking collectives: 63.2 us -> none  [shards(): a_full = lax.all_gather(proj_a, 'narrow', axis=0, tiled=True)]
    dot_general x5 -> x0, matrix products: 44.2 us -> none  [the longest x1 16.9 us: reduce_for_b(): jnp.einsum('ijce,sci->sej', grad_outer, a_full, preferred_element_type=jn...]
    all_gather x1 -> x0, waiting for transfers between devices: 43.9 us -> none  [shards(): b_full = lax.all_gather(proj_b, 'wide', axis=0, tiled=True)]
    ppermute x0 -> x28, starting transfers between devices: none -> 41 us  [the longest x6 16.4 us: send_z(): return lax.ppermute(v, 'wide', wide_perm(k, 0, 0))]
    convert_element_type x2 -> x0, local copies, waits for them, and re-layouts: 24.2 us -> none  [the longest x1 12.3 us: shards(): (summed * scale).astype(jnp.bfloat16).reshape(rows, cols, chans * chans)]
    pallas_call x0 -> x4, Pallas kernels: none -> 21 us  [the longest x1 6.98 us: pair_update(): pl.pallas_call(update_kernel, grid=(ROWS // step,), in_specs=[pl.BlockSpe...]
    ppermute x0 -> x28, waiting for transfers between devices: none -> 6.61 us  [the longest x6 4.11 us: send_z(): return lax.ppermute(v, 'wide', wide_perm(k, 0, 0))]
  transfers between devices with their start and end apart: 3 -> 28, of which waited for: 2 -> 3; matrix products, arithmetic and copies ran while one was open for 26% -> 8% of each run, Pallas kernels for 0% -> 25%
where the time goes in v1:
time: 86.3 us; the launch traced here: 85 us
  starting transfers between devices  41 us (48%)
  Pallas kernels  21 us (24%)
  local copies, waits for them, and re-layouts  13.9 us (16%)
  waiting for transfers between devices  6.61 us (8%)
  other arithmetic  1.52 us (2%)
  between operations  0.93 us (1%)
    ppermute x6, starting transfers between devices, send_z(): return lax.ppermute(v, 'wide', wide_perm(k, 0, 0))  16.4 us
    unnamed x26, local copies, waits for them, and re-layouts  9.19 us
    ppermute x6, starting transfers between devices, send_y(): return lax.ppermute(v, 'wide', wide_perm(0, k, 0))  9.12 us
    pallas_call x1, Pallas kernels, pair_update(): pl.pallas_call(update_kernel, grid=(ROWS // step,), in_specs=[pl.BlockSpe...  6.98 us
    ppermute x6, starting transfers between devices, send_x(): return lax.ppermute(v, 'narrow', narrow_perm(k, 0))  6.94 us
    ppermute x8, starting transfers between devices, send_core(): return lax.ppermute(v, 'wide', wide_perm(0, 0, 1))  6.51 us
    pallas_call x1, Pallas kernels, grad_b_terms(): pl.pallas_call(grad_b_kernel, grid=(C * COLS // step,), in_specs=[pl.Bloc...  5.37 us
    pallas_call x1, Pallas kernels, grad_a_terms(): pl.pallas_call(grad_a_kernel, grid=(ROWS * C // step,), in_specs=[pl.Bloc...  4.59 us
  transfers between devices with their start and end apart: 28, of which 3 were waited for; matrix products, arithmetic and copies ran while one was open for 8% of the time, Pallas kernels for 25%

profile of v1, /device:TPU:1, one launch (start us, length us, event | category | flops | bytes accessed | tf_op | source)
XLA Modules:
  0.0 85.0 jit_solution(5941314821803650901)
XLA Ops:
  1.6 6.9 %collective-permute-start.4 = (bf16[8,4096]{1,0:T(8,128)(2,1)S(1)}, bf16[8,4096]{1,0:T(8,128)(2,1)S(1)}, u32[]{:S(2)}, u32[]{:S(2)}) collective-permute-start(bf16[8,4096]{1,0:T(8,128)(2,1)S(1)} %bitcast.30), channel_id=1, source_target_pairs={{0,192},{8,200},{16,208},{24,216},{32,224},{40,232},{48,240},{56,2... | collective-permute-start | bytes 196616 | tf_op jit(solution)/shard_map/ppermute | solution.py:34
  9.5 2.3 %collective-permute-start.6 = (bf16[8,4096]{1,0:T(8,128)(2,1)S(1)}, bf16[8,4096]{1,0:T(8,128)(2,1)S(1)}, u32[]{:S(2)}, u32[]{:S(2)}) collective-permute-start(bf16[8,4096]{1,0:T(8,128)(2,1)S(1)} %bitcast.32), channel_id=1, source_target_pairs={{0,64},{8,72},{16,80},{24,88},{32,96},{40,104},{48,112},{56,120},{... | collective-permute-start | bytes 196616 | tf_op jit(solution)/shard_map/ppermute | solution.py:34
  11.8 1.1 %copy.17 = bf16[32,32,32]{2,1,0:T(8,128)(2,1)S(1)} copy(bf16[32,32,32]{1,2,0:T(8,128)(2,1)} %bitcast.25) | data formatting | bytes 131072 | tf_op jit(solution)/shard_map/transpose | solution.py:209
  14.9 1.1 %copy.18 = bf16[32,32,128]{2,1,0:T(8,128)(2,1)S(1)} copy(bf16[32,32,128]{2,0,1:T(8,128)(2,1)} %bitcast.26) | data formatting | bytes 524288 | tf_op jit(solution)/shard_map/transpose | solution.py:219
  16.7 2.5 %collective-permute-start.1 = (bf16[64,1024]{1,0:T(8,128)(2,1)S(1)}, bf16[64,1024]{1,0:T(8,128)(2,1)S(1)}, u32[]{:S(2)}, u32[]{:S(2)}) collective-permute-start(bf16[64,1024]{1,0:T(8,128)(2,1)S(1)} %constant_dynamic-update-slice_fusion.x0), channel_id=1, source_target_pairs={{0,6},{1,7},{2,0},{3,1},{4,2},{5,3},{6,4},{7,5},{8,14},{9,15},{10,... | collective-permute-start | bytes 393224 | tf_op jit(solution)/shard_map/ppermute | solution.py:46
  20.3 2.8 %collective-permute-start.7 = (bf16[32,4096]{1,0:T(8,128)(2,1)S(1)}, bf16[32,4096]{1,0:T(8,128)(2,1)S(1)}, u32[]{:S(2)}, u32[]{:S(2)}) collective-permute-start(bf16[32,4096]{1,0:T(8,128)(2,1)S(1)} %constant_dynamic-update-slice_fusion.2.b0), channel_id=1, source_target_pairs={{0,48},{8,56},{16,0},{24,8},{32,16},{40,24},{48,32},{56,40},{64,11... | collective-permute-start | bytes 786440 | tf_op jit(solution)/shard_map/ppermute | solution.py:38
  24.2 4.1 %grad_outer.1.g = bf16[1024,4096]{1,0:T(8,128)(2,1)S(1)} custom-call(bf16[32,128,128]{2,1,0:T(8,128)(2,1)S(1)} %copy-done.2, bf16[1024,128]{1,0:T(8,128)(2,1)S(1)} %bitcast.21), custom_call_target="tpu_custom_call" | custom-call | flops 1073741824 | bytes 9437184 | tf_op jit(solution)/shard_map/grad_outer/pallas_call | solution.py:73
  28.3 4.1 %collective-permute-start.10 = (bf16[32,4096]{1,0:T(8,128)(2,1)S(1)}, bf16[32,4096]{1,0:T(8,128)(2,1)S(1)}, u32[]{:S(2)}, u32[]{:S(2)}) collective-permute-start(bf16[32,4096]{1,0:T(8,128)(2,1)S(1)} %constant_dynamic-update-slice_fusion.2.b0), channel_id=1, source_target_pairs={{0,8},{8,0},{16,24},{24,16},{32,40},{40,32},{48,56},{56,48},{64,72... | collective-permute-start | bytes 786440 | tf_op jit(solution)/shard_map/ppermute | solution.py:42
  32.4 5.4 %grad_b_terms.1 = (f32[128,4096]{1,0:T(8,128)S(1)}, bf16[128,4096]{1,0:T(8,128)(2,1)S(1)}, bf16[1024,256]{1,0:T(8,128)(2,1)S(1)}) custom-call(s32[5]{0:T(128)S(1)} %stack.23.place, bf16[64,1024]{1,0:T(8,128)(2,1)S(1)} %constant_dynamic-update-slice_fusion.x0, bf16[64,1024]{1,0:T(8,128)(2,1)S(1)} %collective-permute-done.1.x1, ...), custom_call_target="tpu_custom_call" | custom-call | flops 2147483648 | bytes 12582912 | tf_op jit(solution)/shard_map/grad_b_terms/pallas_call | solution.py:111
  39.1 1.0 %fusion.8 = (bf16[32,4096]{1,0:T(8,128)(2,1)}, bf16[32,4096]{1,0:T(8,128)(2,1)}, bf16[32,4096]{1,0:T(8,128)(2,1)}, bf16[32,4096]{1,0:T(8,128)(2,1)}) fusion(bf16[128,4096]{1,0:T(8,128)(2,1)S(1)} %get-tuple-element.16), kind=kLoop, calls=%fused_computation.23 | loop fusion | bytes 2097152 | tf_op jit(solution)/shard_map/slice | solution.py:226
  42.8 3.4 %copy-done.1 = bf16[1024,4096]{1,0:T(8,128)(2,1)S(1)} copy-done((bf16[1024,4096]{1,0:T(8,128)(2,1)S(1)}, bf16[1024,4096]{1,0:T(8,128)(2,1)}, u32[]{:S(2)}) %copy-start.1) | copy-done | bytes 8388632
  48.1 4.6 %grad_a_terms.1 = (f32[64,1024]{1,0:T(8,128)S(1)}, bf16[64,1024]{1,0:T(8,128)(2,1)S(1)}, bf16[64,1024]{1,0:T(8,128)(2,1)S(1)}, bf16[64,1024]{1,0:T(8,128)(2,1)S(1)}) custom-call(s32[5]{0:T(128)S(1)} %stack.23.place, bf16[32,4096]{1,0:T(8,128)(2,1)S(1)} %constant_dynamic-update-slice_fusion.2.b0, bf16[32,4096]{1,0:T(8,128)(2,1)S(1)} %collective-permute-done.7.b1, ...), custom_call_target="tpu_custom_call" | custom-call | flops 2147483648 | bytes 12582912 | tf_op jit(solution)/shard_map/grad_a_terms/pallas_call | solution.py:152
  52.7 1.6 %collective-permute-start.14 = (bf16[64,1024]{1,0:T(8,128)(2,1)S(1)}, bf16[64,1024]{1,0:T(8,128)(2,1)S(1)}, u32[]{:S(2)}, u32[]{:S(2)}) collective-permute-start(bf16[64,1024]{1,0:T(8,128)(2,1)S(1)} %get-tuple-element.12), channel_id=1, source_target_pairs={{0,2},{1,3},{2,4},{3,5},{4,6},{5,7},{6,0},{7,1},{8,10},{9,11},{10,... | collective-permute-start | bytes 393224 | tf_op jit(solution)/shard_map/ppermute | solution.py:46
  54.3 1.7 %collective-permute-start.15 = (bf16[64,1024]{1,0:T(8,128)(2,1)S(1)}, bf16[64,1024]{1,0:T(8,128)(2,1)S(1)}, u32[]{:S(2)}, u32[]{:S(2)}) collective-permute-start(bf16[64,1024]{1,0:T(8,128)(2,1)S(1)} %get-tuple-element.13), channel_id=1, source_target_pairs={{0,4},{1,5},{2,6},{3,7},{4,0},{5,1},{6,2},{7,3},{8,12},{9,13},{10,... | collective-permute-start | bytes 393224 | tf_op jit(solution)/shard_map/ppermute | solution.py:46
  56.1 1.2 %add_convert_fusion.2 = (bf16[32,4096]{1,0:T(8,128)(2,1)S(1)}, bf16[32,4096]{1,0:T(8,128)(2,1)S(1)}, bf16[32,4096]{1,0:T(8,128)(2,1)S(1)}) fusion(bf16[32,4096]{1,0:T(8,128)(2,1)} %collective-permute-done.19, f32[128,4096]{1,0:T(8,128)S(1)} %get-tuple-element.15, bf16[32,4096]{1,0:T(8,128)(2,1)} %collective-permute-done.23, ...), kind=kLoop, calls=%fused_computation.3 | loop fusion | flops 1179648 | bytes 3145728 | tf_op jit(solution)/shard_map/convert_element_type | solution.py:229
  57.3 2.6 %collective-permute-start.20 = (bf16[32,4096]{1,0:T(8,128)(2,1)S(1)}, bf16[32,4096]{1,0:T(8,128)(2,1)S(1)}, u32[]{:S(2)}, u32[]{:S(2)}) collective-permute-start(bf16[32,4096]{1,0:T(8,128)(2,1)S(1)} %get-tuple-element.28), channel_id=1, source_target_pairs={{0,32},{8,40},{16,48},{24,56},{32,0},{40,8},{48,16},{56,24},{64,96... | collective-permute-start | bytes 786440 | tf_op jit(solution)/shard_map/ppermute | solution.py:38
  59.9 2.7 %collective-permute-start.24 = (bf16[32,4096]{1,0:T(8,128)(2,1)S(1)}, bf16[32,4096]{1,0:T(8,128)(2,1)S(1)}, u32[]{:S(2)}, u32[]{:S(2)}) collective-permute-start(bf16[32,4096]{1,0:T(8,128)(2,1)S(1)} %get-tuple-element.29), channel_id=1, source_target_pairs={{0,48},{8,56},{16,0},{24,8},{32,16},{40,24},{48,32},{56,40},{64,11... | collective-permute-start | bytes 786440 | tf_op jit(solution)/shard_map/ppermute | solution.py:38
  62.6 7.0 %pair_update.1 = bf16[32,128,128]{2,1,0:T(8,128)(2,1)} custom-call(bf16[1024,256]{1,0:T(8,128)(2,1)S(1)} %copy-done.8, bf16[32,4096]{1,0:T(8,128)(2,1)S(1)} %constant_dynamic-update-slice_fusion.2.b0, bf16[32,4096]{1,0:T(8,128)(2,1)S(1)} %collective-permute-done.7.b1, bf16[32,4096]{1,0:T(8,128)(2,1)S(1)} %collective-permute-done.8.b2, ...), custom_call_target="tpu_custom_call" | custom-call | flops 3221225472 | bytes 4194304 | tf_op jit(solution)/shard_map/pair_update/pallas_call | solution.py:190
  69.7 1.2 %collective-permute-start.17 = (bf16[32,1024]{1,0:T(8,128)(2,1)S(1)}, bf16[32,1024]{1,0:T(8,128)(2,1)S(1)}, u32[]{:S(2)}, u32[]{:S(2)}) collective-permute-start(bf16[32,1024]{1,0:T(8,128)(2,1)S(1)} %slice.87), channel_id=1, source_target_pairs={{0,1},{1,0},{2,3},{3,2},{4,5},{5,4},{6,7},{7,6},{8,9},{9,8},{10,11... | collective-permute-start | bytes 196616 | tf_op jit(solution)/shard_map/ppermute | solution.py:50
  70.9 1.9 %collective-permute-done.22 = bf16[32,4096]{1,0:T(8,128)(2,1)S(1)} collective-permute-done((bf16[32,4096]{1,0:T(8,128)(2,1)S(1)}, bf16[32,4096]{1,0:T(8,128)(2,1)S(1)}, u32[]{:S(2)}, u32[]{:S(2)}) %collective-permute-start.22) | collective-permute-done | bytes 262176 | tf_op jit(solution)/shard_map/ppermute | solution.py:38
  72.9 2.3 %collective-permute-start.25 = (bf16[8,4096]{1,0:T(8,128)(2,1)S(1)}, bf16[8,4096]{1,0:T(8,128)(2,1)S(1)}, u32[]{:S(2)}, u32[]{:S(2)}) collective-permute-start(bf16[8,4096]{1,0:T(8,128)(2,1)S(1)} %get-tuple-element.35), channel_id=1, source_target_pairs={{0,64},{8,72},{16,80},{24,88},{32,96},{40,104},{48,112},{56,120},{... | collective-permute-start | bytes 196616 | tf_op jit(solution)/shard_map/ppermute | solution.py:34
  75.2 1.8 %collective-permute-start.26 = (bf16[8,4096]{1,0:T(8,128)(2,1)S(1)}, bf16[8,4096]{1,0:T(8,128)(2,1)S(1)}, u32[]{:S(2)}, u32[]{:S(2)}) collective-permute-start(bf16[8,4096]{1,0:T(8,128)(2,1)S(1)} %get-tuple-element.37), channel_id=1, source_target_pairs={{0,128},{8,136},{16,144},{24,152},{32,160},{40,168},{48,176},{56,1... | collective-permute-start | bytes 196616 | tf_op jit(solution)/shard_map/ppermute | solution.py:34
  77.0 2.1 %collective-permute-start.27 = (bf16[8,4096]{1,0:T(8,128)(2,1)S(1)}, bf16[8,4096]{1,0:T(8,128)(2,1)S(1)}, u32[]{:S(2)}, u32[]{:S(2)}) collective-permute-start(bf16[8,4096]{1,0:T(8,128)(2,1)S(1)} %get-tuple-element.36), channel_id=1, source_target_pairs={{0,192},{8,200},{16,208},{24,216},{32,224},{40,232},{48,240},{56,2... | collective-permute-start | bytes 196616 | tf_op jit(solution)/shard_map/ppermute | solution.py:34
  80.2 4.1 %collective-permute-done.26 = bf16[8,4096]{1,0:T(8,128)(2,1)S(1)} collective-permute-done((bf16[8,4096]{1,0:T(8,128)(2,1)S(1)}, bf16[8,4096]{1,0:T(8,128)(2,1)S(1)}, u32[]{:S(2)}, u32[]{:S(2)}) %collective-permute-start.26) | collective-permute-done | bytes 65568 | tf_op jit(solution)/shard_map/ppermute | solution.py:34
  (79 shorter events, 14.7 us)
Async XLA Ops:
  1.6 18.1 %collective-permute-start.4 = (bf16[8,4096]{1,0:T(8,128)(2,1)S(1)}, bf16[8,4096]{1,0:T(8,128)(2,1)S(1)}, u32[]{:S(2)}, u32[]{:S(2)}) collective-permute-start(bf16[8,4096]{1,0:T(8,128)(2,1)S(1)} %bitcast.30), channel_id=1, source_target_pairs={{0,192},{8,200},{16,208},{24,216},{32,224},{40,232},{48,240},{56,2... | collective-permute-start | bytes 196616 | tf_op jit(solution)/shard_map/ppermute | solution.py:34
  8.5 11.8 %collective-permute-start.5 = (bf16[8,4096]{1,0:T(8,128)(2,1)S(1)}, bf16[8,4096]{1,0:T(8,128)(2,1)S(1)}, u32[]{:S(2)}, u32[]{:S(2)}) collective-permute-start(bf16[8,4096]{1,0:T(8,128)(2,1)S(1)} %bitcast.31), channel_id=1, source_target_pairs={{0,128},{8,136},{16,144},{24,152},{32,160},{40,168},{48,176},{56,1... | collective-permute-start | bytes 196616 | tf_op jit(solution)/shard_map/ppermute | solution.py:34
  9.5 10.8 %collective-permute-start.6 = (bf16[8,4096]{1,0:T(8,128)(2,1)S(1)}, bf16[8,4096]{1,0:T(8,128)(2,1)S(1)}, u32[]{:S(2)}, u32[]{:S(2)}) collective-permute-start(bf16[8,4096]{1,0:T(8,128)(2,1)S(1)} %bitcast.32), channel_id=1, source_target_pairs={{0,64},{8,72},{16,80},{24,88},{32,96},{40,104},{48,112},{56,120},{... | collective-permute-start | bytes 196616 | tf_op jit(solution)/shard_map/ppermute | solution.py:34
  16.7 6.8 %collective-permute-start.1 = (bf16[64,1024]{1,0:T(8,128)(2,1)S(1)}, bf16[64,1024]{1,0:T(8,128)(2,1)S(1)}, u32[]{:S(2)}, u32[]{:S(2)}) collective-permute-start(bf16[64,1024]{1,0:T(8,128)(2,1)S(1)} %constant_dynamic-update-slice_fusion.x0), channel_id=1, source_target_pairs={{0,6},{1,7},{2,0},{3,1},{4,2},{5,3},{6,4},{7,5},{8,14},{9,15},{10,... | collective-permute-start | bytes 393224 | tf_op jit(solution)/shard_map/ppermute | solution.py:46
  19.2 9.1 %collective-permute-start.2 = (bf16[64,1024]{1,0:T(8,128)(2,1)S(1)}, bf16[64,1024]{1,0:T(8,128)(2,1)S(1)}, u32[]{:S(2)}, u32[]{:S(2)}) collective-permute-start(bf16[64,1024]{1,0:T(8,128)(2,1)S(1)} %constant_dynamic-update-slice_fusion.x0), channel_id=1, source_target_pairs={{0,4},{1,5},{2,6},{3,7},{4,0},{5,1},{6,2},{7,3},{8,12},{9,13},{10,... | collective-permute-start | bytes 393224 | tf_op jit(solution)/shard_map/ppermute | solution.py:46
  19.7 12.7 %collective-permute-start.3 = (bf16[64,1024]{1,0:T(8,128)(2,1)S(1)}, bf16[64,1024]{1,0:T(8,128)(2,1)S(1)}, u32[]{:S(2)}, u32[]{:S(2)}) collective-permute-start(bf16[64,1024]{1,0:T(8,128)(2,1)S(1)} %constant_dynamic-update-slice_fusion.x0), channel_id=1, source_target_pairs={{0,2},{1,3},{2,4},{3,5},{4,6},{5,7},{6,0},{7,1},{8,10},{9,11},{10,... | collective-permute-start | bytes 393224 | tf_op jit(solution)/shard_map/ppermute | solution.py:46
  20.3 17.5 %collective-permute-start.7 = (bf16[32,4096]{1,0:T(8,128)(2,1)S(1)}, bf16[32,4096]{1,0:T(8,128)(2,1)S(1)}, u32[]{:S(2)}, u32[]{:S(2)}) collective-permute-start(bf16[32,4096]{1,0:T(8,128)(2,1)S(1)} %constant_dynamic-update-slice_fusion.2.b0), channel_id=1, source_target_pairs={{0,48},{8,56},{16,0},{24,8},{32,16},{40,24},{48,32},{56,40},{64,11... | collective-permute-start | bytes 786440 | tf_op jit(solution)/shard_map/ppermute | solution.py:38
  23.2 14.8 %collective-permute-start.8 = (bf16[32,4096]{1,0:T(8,128)(2,1)S(1)}, bf16[32,4096]{1,0:T(8,128)(2,1)S(1)}, u32[]{:S(2)}, u32[]{:S(2)}) collective-permute-start(bf16[32,4096]{1,0:T(8,128)(2,1)S(1)} %constant_dynamic-update-slice_fusion.2.b0), channel_id=1, source_target_pairs={{0,32},{8,40},{16,48},{24,56},{32,0},{40,8},{48,16},{56,24},{64,96... | collective-permute-start | bytes 786440 | tf_op jit(solution)/shard_map/ppermute | solution.py:38
  23.5 14.9 %collective-permute-start.9 = (bf16[32,4096]{1,0:T(8,128)(2,1)S(1)}, bf16[32,4096]{1,0:T(8,128)(2,1)}, u32[]{:S(2)}, u32[]{:S(2)}) collective-permute-start(bf16[32,4096]{1,0:T(8,128)(2,1)S(1)} %constant_dynamic-update-slice_fusion.2.b0), channel_id=1, source_target_pairs={{0,16},{8,24},{16,32},{24,40},{32,48},{40,56},{48,0},{56,8},{64,80... | collective-permute-start | bytes 786440 | tf_op jit(solution)/shard_map/ppermute | solution.py:38
  28.3 11.8 %collective-permute-start.10 = (bf16[32,4096]{1,0:T(8,128)(2,1)S(1)}, bf16[32,4096]{1,0:T(8,128)(2,1)S(1)}, u32[]{:S(2)}, u32[]{:S(2)}) collective-permute-start(bf16[32,4096]{1,0:T(8,128)(2,1)S(1)} %constant_dynamic-update-slice_fusion.2.b0), channel_id=1, source_target_pairs={{0,8},{8,0},{16,24},{24,16},{32,40},{40,32},{48,56},{56,48},{64,72... | collective-permute-start | bytes 786440 | tf_op jit(solution)/shard_map/ppermute | solution.py:42
  40.1 14.2 %collective-permute-start.19 = (bf16[32,4096]{1,0:T(8,128)(2,1)}, bf16[32,4096]{1,0:T(8,128)(2,1)}, u32[]{:S(2)}, u32[]{:S(2)}) collective-permute-start(bf16[32,4096]{1,0:T(8,128)(2,1)} %get-tuple-element.34), channel_id=1, source_target_pairs={{0,8},{8,0},{16,24},{24,16},{32,40},{40,32},{48,56},{56,48},{64,72... | collective-permute-start | bytes 786440 | tf_op jit(solution)/shard_map/ppermute | solution.py:42
  40.8 15.2 %collective-permute-start.21 = (bf16[32,4096]{1,0:T(8,128)(2,1)}, bf16[32,4096]{1,0:T(8,128)(2,1)}, u32[]{:S(2)}, u32[]{:S(2)}) collective-permute-start(bf16[32,4096]{1,0:T(8,128)(2,1)} %get-tuple-element.33), channel_id=1, source_target_pairs={{0,8},{8,0},{16,24},{24,16},{32,40},{40,32},{48,56},{56,48},{64,72... | collective-permute-start | bytes 786440 | tf_op jit(solution)/shard_map/ppermute | solution.py:42
  42.0 14.0 %collective-permute-start.23 = (bf16[32,4096]{1,0:T(8,128)(2,1)}, bf16[32,4096]{1,0:T(8,128)(2,1)}, u32[]{:S(2)}, u32[]{:S(2)}) collective-permute-start(bf16[32,4096]{1,0:T(8,128)(2,1)} %get-tuple-element.32), channel_id=1, source_target_pairs={{0,8},{8,0},{16,24},{24,16},{32,40},{40,32},{48,56},{56,48},{64,72... | collective-permute-start | bytes 786440 | tf_op jit(solution)/shard_map/ppermute | solution.py:42
  42.2 28.7 %collective-permute-start.18 = (bf16[32,4096]{1,0:T(8,128)(2,1)}, bf16[32,4096]{1,0:T(8,128)(2,1)S(1)}, u32[]{:S(2)}, u32[]{:S(2)}) collective-permute-start(bf16[32,4096]{1,0:T(8,128)(2,1)} %get-tuple-element.31), channel_id=1, source_target_pairs={{0,8},{8,0},{16,24},{24,16},{32,40},{40,32},{48,56},{56,48},{64,72... | collective-permute-start | bytes 786440 | tf_op jit(solution)/shard_map/ppermute | solution.py:42
  52.7 7.2 %collective-permute-start.14 = (bf16[64,1024]{1,0:T(8,128)(2,1)S(1)}, bf16[64,1024]{1,0:T(8,128)(2,1)S(1)}, u32[]{:S(2)}, u32[]{:S(2)}) collective-permute-start(bf16[64,1024]{1,0:T(8,128)(2,1)S(1)} %get-tuple-element.12), channel_id=1, source_target_pairs={{0,2},{1,3},{2,4},{3,5},{4,6},{5,7},{6,0},{7,1},{8,10},{9,11},{10,... | collective-permute-start | bytes 393224 | tf_op jit(solution)/shard_map/ppermute | solution.py:46
  54.3 8.3 %collective-permute-start.15 = (bf16[64,1024]{1,0:T(8,128)(2,1)S(1)}, bf16[64,1024]{1,0:T(8,128)(2,1)S(1)}, u32[]{:S(2)}, u32[]{:S(2)}) collective-permute-start(bf16[64,1024]{1,0:T(8,128)(2,1)S(1)} %get-tuple-element.13), channel_id=1, source_target_pairs={{0,4},{1,5},{2,6},{3,7},{4,0},{5,1},{6,2},{7,3},{8,12},{9,13},{10,... | collective-permute-start | bytes 393224 | tf_op jit(solution)/shard_map/ppermute | solution.py:46
  57.3 13.6 %collective-permute-start.20 = (bf16[32,4096]{1,0:T(8,128)(2,1)S(1)}, bf16[32,4096]{1,0:T(8,128)(2,1)S(1)}, u32[]{:S(2)}, u32[]{:S(2)}) collective-permute-start(bf16[32,4096]{1,0:T(8,128)(2,1)S(1)} %get-tuple-element.28), channel_id=1, source_target_pairs={{0,32},{8,40},{16,48},{24,56},{32,0},{40,8},{48,16},{56,24},{64,96... | collective-permute-start | bytes 786440 | tf_op jit(solution)/shard_map/ppermute | solution.py:38
  59.9 12.8 %collective-permute-start.22 = (bf16[32,4096]{1,0:T(8,128)(2,1)S(1)}, bf16[32,4096]{1,0:T(8,128)(2,1)S(1)}, u32[]{:S(2)}, u32[]{:S(2)}) collective-permute-start(bf16[32,4096]{1,0:T(8,128)(2,1)S(1)} %get-tuple-element.30), channel_id=1, source_target_pairs={{0,16},{8,24},{16,32},{24,40},{32,48},{40,56},{48,0},{56,8},{64,80... | collective-permute-start | bytes 786440 | tf_op jit(solution)/shard_map/ppermute | solution.py:38
  59.9 12.8 %collective-permute-start.24 = (bf16[32,4096]{1,0:T(8,128)(2,1)S(1)}, bf16[32,4096]{1,0:T(8,128)(2,1)S(1)}, u32[]{:S(2)}, u32[]{:S(2)}) collective-permute-start(bf16[32,4096]{1,0:T(8,128)(2,1)S(1)} %get-tuple-element.29), channel_id=1, source_target_pairs={{0,48},{8,56},{16,0},{24,8},{32,16},{40,24},{48,32},{56,40},{64,11... | collective-permute-start | bytes 786440 | tf_op jit(solution)/shard_map/ppermute | solution.py:38
  62.6 7.0 %collective-permute-start.16 = (bf16[64,1024]{1,0:T(8,128)(2,1)S(1)}, bf16[64,1024]{1,0:T(8,128)(2,1)S(1)}, u32[]{:S(2)}, u32[]{:S(2)}) collective-permute-start(bf16[64,1024]{1,0:T(8,128)(2,1)S(1)} %get-tuple-element.14), channel_id=1, source_target_pairs={{0,6},{1,7},{2,0},{3,1},{4,2},{5,3},{6,4},{7,5},{8,14},{9,15},{10,... | collective-permute-start | bytes 393224 | tf_op jit(solution)/shard_map/ppermute | solution.py:46
  69.7 9.5 %collective-permute-start.17 = (bf16[32,1024]{1,0:T(8,128)(2,1)S(1)}, bf16[32,1024]{1,0:T(8,128)(2,1)S(1)}, u32[]{:S(2)}, u32[]{:S(2)}) collective-permute-start(bf16[32,1024]{1,0:T(8,128)(2,1)S(1)} %slice.87), channel_id=1, source_target_pairs={{0,1},{1,0},{2,3},{3,2},{4,5},{5,4},{6,7},{7,6},{8,9},{9,8},{10,11... | collective-permute-start | bytes 196616 | tf_op jit(solution)/shard_map/ppermute | solution.py:50
  72.9 7.3 %collective-permute-start.25 = (bf16[8,4096]{1,0:T(8,128)(2,1)S(1)}, bf16[8,4096]{1,0:T(8,128)(2,1)S(1)}, u32[]{:S(2)}, u32[]{:S(2)}) collective-permute-start(bf16[8,4096]{1,0:T(8,128)(2,1)S(1)} %get-tuple-element.35), channel_id=1, source_target_pairs={{0,64},{8,72},{16,80},{24,88},{32,96},{40,104},{48,112},{56,120},{... | collective-permute-start | bytes 196616 | tf_op jit(solution)/shard_map/ppermute | solution.py:34
  75.2 9.1 %collective-permute-start.26 = (bf16[8,4096]{1,0:T(8,128)(2,1)S(1)}, bf16[8,4096]{1,0:T(8,128)(2,1)S(1)}, u32[]{:S(2)}, u32[]{:S(2)}) collective-permute-start(bf16[8,4096]{1,0:T(8,128)(2,1)S(1)} %get-tuple-element.37), channel_id=1, source_target_pairs={{0,128},{8,136},{16,144},{24,152},{32,160},{40,168},{48,176},{56,1... | collective-permute-start | bytes 196616 | tf_op jit(solution)/shard_map/ppermute | solution.py:34
  77.0 7.3 %collective-permute-start.27 = (bf16[8,4096]{1,0:T(8,128)(2,1)S(1)}, bf16[8,4096]{1,0:T(8,128)(2,1)S(1)}, u32[]{:S(2)}, u32[]{:S(2)}) collective-permute-start(bf16[8,4096]{1,0:T(8,128)(2,1)S(1)} %get-tuple-element.36), channel_id=1, source_target_pairs={{0,192},{8,200},{16,208},{24,216},{32,224},{40,232},{48,240},{56,2... | collective-permute-start | bytes 196616 | tf_op jit(solution)/shard_map/ppermute | solution.py:34
  (14 other events, 79.4 us)

commit v2 on v1

v2 whole, which is shorter than its diff:
```python
import jax
import jax.numpy as jnp
from jax import lax
from jax.experimental import pallas as pl
from jax.experimental.pallas import tpu as pltpu
from jax.sharding import PartitionSpec as P

F32 = jnp.float32
BF16 = jnp.bfloat16
C = 32
K = 128
SEQ = 256
ROWS = 32
COLS = 128
SCALE = 1.0 / SEQ
MIB = 1024 * 1024


def wide_perm(dz, dy, dc):
    perm = []
    for w in range(32):
        z, y, c = w // 8, (w // 2) % 4, w % 2
        perm.append((w, ((z ^ dz) * 4 + (y + dy) % 4) * 2 + (c ^ dc)))
    return perm


def narrow_perm(dx, dl):
    return [(n, ((n // 2) ^ dx) * 2 + ((n % 2) ^ dl)) for n in range(8)]


def swap_z(v, d):
    return lax.ppermute(v, "wide", wide_perm(d, 0, 0))


def send_y(v, k):
    return lax.ppermute(v, "wide", wide_perm(0, k, 0))


def swap_core(v):
    return lax.ppermute(v, "wide", wide_perm(0, 0, 1))


def swap_x(v, d):
    return lax.ppermute(v, "narrow", narrow_perm(d, 0))


def swap_l(v):
    return lax.ppermute(v, "narrow", narrow_perm(0, 1))


def both(v, w):
    return jnp.concatenate([v, w], 0)


def own_row(place, qx, rl, yl, core):
    z, y, c, x, l = (place[q] for q in range(5))
    d = (x ^ (0, 1, 3, 2)[qx]) ^ z
    zz = d ^ (d >> 1)
    yy = lax.rem(2 * (l ^ rl) + yl - y + 4, 4)
    cc = core ^ c
    return pl.multiple_of(((cc * 4 + yy) * 4 + zz) * 8, 8)


def grad_outer_kernel(cot, w, g, wt, wide, wp):
    @pl.when(pl.program_id(0) == 0)
    def _():
        wide[...] = w[...].astype(F32)
        for e in range(C):
            wp[e * C:(e + 1) * C, :] = wide[pl.ds(e, C, stride=C), :].astype(BF16)
        wt[...] = wp[...].T

    count = cot.shape[0]
    rows = cot[...].reshape(count * COLS, K)
    r = lax.dot_general(wp[...], rows, (((1,), (1,)), ((), ())), preferred_element_type=F32)
    r = r.astype(BF16)
    for i in range(count):
        for e in range(C):
            g[pl.ds(pl.multiple_of((pl.program_id(0) * count + i) * C, C), C), e * COLS:(e + 1) * COLS] = r[e * C:(e + 1) * C, i * COLS:(i + 1) * COLS]


def grad_outer(cot, w):
    step = 32
    return pl.pallas_call(
        grad_outer_kernel,
        grid=(ROWS // step,),
        in_specs=[
            pl.BlockSpec((step, COLS, K), lambda r: (r, 0, 0)),
            pl.BlockSpec((C * C, K), lambda r: (0, 0)),
        ],
        out_specs=[
            pl.BlockSpec(memory_space=pltpu.VMEM),
            pl.BlockSpec((K, C * C), lambda r: (0, 0)),
        ],
        out_shape=[
            pltpu.VMEM((ROWS * C, C * COLS), BF16),
            jax.ShapeDtypeStruct((K, C * C), BF16),
        ],
        scratch_shapes=[pltpu.VMEM((C * C, K), F32), pltpu.VMEM((C * C, K), BF16)],
        compiler_params=pltpu.CompilerParams(vmem_limit_bytes=24 * MIB),
        cost_estimate=pl.CostEstimate(flops=2 * 4096 * 1024 * 128, bytes_accessed=9 * MIB, transcendentals=0),
        name="grad_outer",
    )(pltpu.with_memory_space_constraint(cot, pltpu.HBM), pltpu.with_memory_space_constraint(w, pltpu.HBM))


def grad_b_kernel(place, x0, x1, g, keep, away, at, order, a):
    if True:
        for qx in range(4):
            v = (x0, x1)[qx // 2][(qx % 2) * 64:(qx % 2 + 1) * 64, :].astype(F32)
            for rl in range(2):
                for yl in range(2):
                    for core in range(2):
                        at_row = ((rl * 2 + yl) * 2 + core) * 8
                        order[pl.ds(own_row(place, qx, rl, yl, core), 8), :] = v[at_row:at_row + 8, :]
        v = order[...]
        a[...] = v.astype(BF16)
        at[...] = v.T.astype(BF16)

    step = 4096

    def body(n, carry):
        cols = pl.ds(pl.multiple_of(n * step, step), step)
        r = jnp.dot(a[...], g[:, cols], preferred_element_type=F32)
        keep[:, cols] = r[:SEQ // 2]
        away[:, cols] = r[SEQ // 2:].astype(BF16)
        return carry

    lax.fori_loop(0, C * COLS // step, body, 0)


def grad_b_terms(place, xs, g):
    half = SEQ // 2
    whole = pl.BlockSpec(memory_space=pltpu.VMEM)
    return pl.pallas_call(
        grad_b_kernel,
        in_specs=[pl.BlockSpec(memory_space=pltpu.SMEM)] + [whole] * 3,
        out_specs=[whole] * 3,
        out_shape=[
            jax.ShapeDtypeStruct((half, C * COLS), F32),
            jax.ShapeDtypeStruct((half, C * COLS), BF16),
            jax.ShapeDtypeStruct((ROWS * C, SEQ), BF16),
        ],
        scratch_shapes=[pltpu.VMEM((SEQ, ROWS * C), F32), pltpu.VMEM((SEQ, ROWS * C), BF16)],
        compiler_params=pltpu.CompilerParams(vmem_limit_bytes=24 * MIB),
        cost_estimate=pl.CostEstimate(flops=2 * 4096 * 1024 * 256, bytes_accessed=12 * MIB, transcendentals=0),
        name="grad_b_terms",
    )(place, *xs, g)


def grad_a_kernel(place, b0, b1, b2, b3, b4, b5, b6, b7, g, keep, away, b, r):
    for q, piece in enumerate((b0, b1, b2, b3, b4, b5, b6, b7)):
        b[q * 32:(q + 1) * 32, :] = piece[...]
    step = 1024

    def body(n, carry):
        at = pl.ds(pl.multiple_of(n * step, step), step)
        r[...] = lax.dot_general(b[...], g[at, :], (((1,), (1,)), ((), ())), preferred_element_type=F32)
        for qx in range(4):
            out = (keep, away)[qx // 2]
            for rl in range(2):
                for yl in range(2):
                    pair = [r[pl.ds(own_row(place, qx, rl, yl, core), 8), :] for core in range(2)]
                    row = (qx % 2) * 64 + (rl * 2 + yl) * 16
                    out[row:row + 16, at] = jnp.concatenate(pair, 0).astype(out.dtype)
        return carry

    lax.fori_loop(0, ROWS * C // step, body, 0)


def grad_a_terms(place, bs, g):
    whole = pl.BlockSpec(memory_space=pltpu.VMEM)
    return pl.pallas_call(
        grad_a_kernel,
        in_specs=[pl.BlockSpec(memory_space=pltpu.SMEM)] + [whole] * 9,
        out_specs=[whole] * 3,
        out_shape=[
            jax.ShapeDtypeStruct((128, ROWS * C), F32),
            jax.ShapeDtypeStruct((128, ROWS * C), BF16),
            jax.ShapeDtypeStruct((SEQ, C * COLS), BF16),
        ],
        scratch_shapes=[pltpu.VMEM((SEQ, 1024), F32)],
        compiler_params=pltpu.CompilerParams(vmem_limit_bytes=24 * MIB),
        cost_estimate=pl.CostEstimate(flops=2 * 4096 * 1024 * 256, bytes_accessed=12 * MIB, transcendentals=0),
        name="grad_a_terms",
    )(place, *bs, g)


def update_kernel(at, b, wt, bias, out, o):
    count = out.shape[0]
    wide = 8
    for start in range(0, C, wide):
        r = jnp.dot(at[...], b[:, start * COLS:(start + wide) * COLS], preferred_element_type=F32)
        r = (r * SCALE).astype(BF16)
        for i in range(count):
            for e in range(wide):
                row = (start + e) * C
                o[row:row + C, i * COLS:(i + 1) * COLS] = r[i * C:(i + 1) * C, e * COLS:(e + 1) * COLS]
    u = jnp.dot(wt[...], o[...], preferred_element_type=F32)
    for i in range(count):
        out[i] = (u[:, i * COLS:(i + 1) * COLS].T + bias[...]).astype(BF16)


def pair_update(at, b, wt, bias):
    step = 32
    return pl.pallas_call(
        update_kernel,
        grid=(ROWS // step,),
        in_specs=[
            pl.BlockSpec((step * C, SEQ), lambda r: (r, 0)),
            pl.BlockSpec((SEQ, C * COLS), lambda r: (0, 0)),
            pl.BlockSpec((K, C * C), lambda r: (0, 0)),
            pl.BlockSpec((1, K), lambda r: (0, 0)),
        ],
        out_specs=pl.BlockSpec((step, COLS, K), lambda r: (r, 0, 0)),
        out_shape=jax.ShapeDtypeStruct((ROWS, COLS, K), BF16),
        scratch_shapes=[pltpu.VMEM((C * C, step * COLS), BF16)],
        compiler_params=pltpu.CompilerParams(vmem_limit_bytes=24 * MIB),
        cost_estimate=pl.CostEstimate(flops=3 * 4096 * 1024 * 256, bytes_accessed=4 * MIB, transcendentals=0),
        name="pair_update",
    )(at, b, wt, bias)


def shards(proj_a, proj_b, out_weight, out_bias, pair_cotangent):
    w = lax.axis_index("wide")
    n = lax.axis_index("narrow")
    place = jnp.stack([w >> 3, (w >> 1) & 3, w & 1, n >> 1, n & 1]).astype(jnp.int32)

    b0 = lax.optimization_barrier(proj_b.reshape(8, C * COLS))
    b1 = both(b0, swap_z(b0, 1))

    a0 = lax.optimization_barrier(proj_a.transpose(0, 2, 1).reshape(32, ROWS * C))
    a1 = both(a0, swap_l(a0))
    a2 = both(a1, swap_x(a1, 1))
    xs = [a2, swap_x(a2, 3)]

    b2 = both(b1, swap_z(b1, 3))
    ys = [b2] + [send_y(b2, -k) for k in (1, 2, 3)]
    bs = ys + [swap_core(v) for v in ys]

    place, pair_cotangent = lax.optimization_barrier((place, pair_cotangent))
    g, weight_t = grad_outer(pair_cotangent, out_weight)

    keep, away, at = grad_b_terms(place, xs, g)
    parts = {}
    for k in (2, 1, 3, 0):
        part = slice(32 * k, 32 * (k + 1))
        parts[k] = keep[part] + swap_core(away[part]).astype(F32)
    total = parts[0]
    for k in (2, 1, 3):
        total = total + send_y(parts[k].astype(BF16), k).astype(F32)
    b_summed = total[:8]
    for q, d in ((3, 2), (1, 1), (2, 3)):
        b_summed = b_summed + swap_z(total[8 * q:8 * (q + 1)].astype(BF16), d).astype(F32)
    grad_b = (b_summed * SCALE).astype(BF16).reshape(8, C, COLS)

    keep, away, b_full = grad_a_terms(place, bs, g)
    total = keep + swap_x(away, 3).astype(F32)
    total = total[:64] + swap_x(total[64:].astype(BF16), 1).astype(F32)
    a_summed = total[:32] + swap_l(total[32:].astype(BF16)).astype(F32)
    grad_a = (a_summed * SCALE).astype(BF16).reshape(32, ROWS, C).transpose(0, 2, 1)

    update = pair_update(at, b_full, weight_t, out_bias.reshape(1, K))
    return (update, grad_a, grad_b)


def solution(mesh):
    placed = (
        P("narrow", None, "wide"),
        P("wide", None, "narrow"),
        P(),
        P(),
        P("wide", "narrow", None),
    )
    return jax.shard_map(
        shards,
        mesh=mesh,
        in_specs=placed,
        out_specs=(P("wide", "narrow", None), P("narrow", None, "wide"), P("wide", None, "narrow")),
        check_vma=False,
    )
```

time: 86.3 us -> 68.9 us (0.80)
  the two profiles are of different devices: /device:TPU:1 before, /device:TPU:4 now
where the time goes in v2:
time: 68.9 us; the launch traced here: 68.7 us
  starting transfers between devices  39.5 us (57%)
  Pallas kernels  15 us (22%)
  waiting for transfers between devices  8.74 us (13%)
  local copies, waits for them, and re-layouts  4.14 us (6%)
  between operations  0.8 us (1%)
    ppermute x5, starting transfers between devices, swap_z(): return lax.ppermute(v, 'wide', wide_perm(d, 0, 0))  14.8 us
    ppermute x6, starting transfers between devices, send_y(): return lax.ppermute(v, 'wide', wide_perm(0, k, 0))  12.1 us
    ppermute x4, starting transfers between devices, swap_x(): return lax.ppermute(v, 'narrow', narrow_perm(d, 0))  5.92 us
    pallas_call x1, Pallas kernels, pair_update(): pl.pallas_call(update_kernel, grid=(ROWS // step,), in_specs=[pl.BlockSpe...  5.06 us
    ppermute x2, starting transfers between devices, swap_l(): return lax.ppermute(v, 'narrow', narrow_perm(0, 1))  5.04 us
    ppermute x5, waiting for transfers between devices, swap_z(): return lax.ppermute(v, 'wide', wide_perm(d, 0, 0))  4.2 us
    pallas_call x1, Pallas kernels, grad_outer(): pl.pallas_call(grad_outer_kernel, grid=(ROWS // step,), in_specs=[pl.Bloc...  3.98 us
    ppermute x6, waiting for transfers between devices, send_y(): return lax.ppermute(v, 'wide', wide_perm(0, k, 0))  3.4 us
  transfers between devices with their start and end apart: 25, of which 6 were waited for; matrix products, arithmetic and copies ran while one was open for 3% of the time, Pallas kernels for 22%

profile of v2, /device:TPU:4, one launch (start us, length us, event | category | flops | bytes accessed | tf_op | source)
XLA Modules:
  0.0 68.7 jit_solution(11812643853221963386)
XLA Ops:
  0.6 1.1 %copy.8 = bf16[32,32,32]{2,1,0:T(8,128)(2,1)S(1)} copy(bf16[32,32,32]{1,2,0:T(8,128)(2,1)} %bitcast.18) | data formatting | bytes 131072 | tf_op jit(solution)/shard_map/transpose | solution.py:230
  2.0 2.0 %collective-permute-start = (bf16[32,1024]{1,0:T(8,128)(2,1)S(1)}, bf16[32,1024]{1,0:T(8,128)(2,1)S(1)}, u32[]{:S(2)}, u32[]{:S(2)}) collective-permute-start(bf16[32,1024]{1,0:T(8,128)(2,1)S(1)} %reshape.21), channel_id=1, source_target_pairs={{0,1},{1,0},{2,3},{3,2},{4,5},{5,4},{6,7},{7,6},{8,9},{9,8},{10,11... | collective-permute-start | bytes 196616 | tf_op jit(solution)/shard_map/ppermute | solution.py:48
  4.0 0.9 %copy.13 = bf16[1,8,32,128]{3,1,2,0:T(8,128)(2,1)S(1)} copy(bf16[1,8,32,128]{3,2,1,0:T(8,128)(2,1)} %bitcast.20) | data formatting | bytes 131072
  4.9 3.4 %collective-permute-start.3 = (bf16[8,4096]{1,0:T(8,128)(2,1)S(1)}, bf16[8,4096]{1,0:T(8,128)(2,1)S(1)}, u32[]{:S(2)}, u32[]{:S(2)}) collective-permute-start(bf16[8,4096]{1,0:T(8,128)(2,1)S(1)} %bitcast.15), channel_id=1, source_target_pairs={{0,64},{8,72},{16,80},{24,88},{32,96},{40,104},{48,112},{56,120},{... | collective-permute-start | bytes 196616 | tf_op jit(solution)/shard_map/ppermute | solution.py:32
  8.4 1.3 %collective-permute-start.1 = (bf16[64,1024]{1,0:T(8,128)(2,1)S(1)}, bf16[64,1024]{1,0:T(8,128)(2,1)S(1)}, u32[]{:S(2)}, u32[]{:S(2)}) collective-permute-start(bf16[64,1024]{1,0:T(8,128)(2,1)S(1)} %pad_maximum_fusion.2), channel_id=1, source_target_pairs={{0,2},{1,3},{2,0},{3,1},{4,6},{5,7},{6,4},{7,5},{8,10},{9,11},{10,... | collective-permute-start | bytes 393224 | tf_op jit(solution)/shard_map/ppermute | solution.py:44
  9.6 1.7 %collective-permute-done.3 = bf16[8,4096]{1,0:T(8,128)(2,1)S(1)} collective-permute-done((bf16[8,4096]{1,0:T(8,128)(2,1)S(1)}, bf16[8,4096]{1,0:T(8,128)(2,1)S(1)}, u32[]{:S(2)}, u32[]{:S(2)}) %collective-permute-start.3) | collective-permute-done | bytes 65568 | tf_op jit(solution)/shard_map/ppermute | solution.py:32
  11.4 4.4 %collective-permute-start.4 = (bf16[16,4096]{1,0:T(8,128)(2,1)S(1)}, bf16[16,4096]{1,0:T(8,128)(2,1)S(1)}, u32[]{:S(2)}, u32[]{:S(2)}) collective-permute-start(bf16[16,4096]{1,0:T(8,128)(2,1)S(1)} %pad_maximum_fusion.3), channel_id=1, source_target_pairs={{0,192},{8,200},{16,208},{24,216},{32,224},{40,232},{48,240},{56,2... | collective-permute-start | bytes 393224 | tf_op jit(solution)/shard_map/ppermute | solution.py:32
  15.7 4.0 %grad_outer.1 = (bf16[1024,4096]{1,0:T(8,128)(2,1)S(1)}, bf16[128,1024]{1,0:T(8,128)(2,1)S(1)}) custom-call(bf16[32,128,128]{2,1,0:T(8,128)(2,1)} %cot, bf16[1024,128]{1,0:T(8,128)(2,1)} %w.1), custom_call_target="tpu_custom_call" | custom-call | flops 1073741824 | bytes 9437184 | tf_op jit(solution)/shard_map/grad_outer/pallas_call | solution.py:83
  20.4 3.3 %collective-permute-start.6 = (bf16[32,4096]{1,0:T(8,128)(2,1)S(1)}, bf16[32,4096]{1,0:T(8,128)(2,1)S(1)}, u32[]{:S(2)}, u32[]{:S(2)}) collective-permute-start(bf16[32,4096]{1,0:T(8,128)(2,1)S(1)} %pad_maximum_fusion.1.b0), channel_id=1, source_target_pairs={{0,32},{8,40},{16,48},{24,56},{32,0},{40,8},{48,16},{56,24},{64,96... | collective-permute-start | bytes 786440 | tf_op jit(solution)/shard_map/ppermute | solution.py:36
  24.4 2.6 %collective-permute-start.5 = (bf16[32,4096]{1,0:T(8,128)(2,1)S(1)}, bf16[32,4096]{1,0:T(8,128)(2,1)S(1)}, u32[]{:S(2)}, u32[]{:S(2)}) collective-permute-start(bf16[32,4096]{1,0:T(8,128)(2,1)S(1)} %pad_maximum_fusion.1.b0), channel_id=1, source_target_pairs={{0,48},{8,56},{16,0},{24,8},{32,16},{40,24},{48,32},{56,40},{64,11... | collective-permute-start | bytes 786440 | tf_op jit(solution)/shard_map/ppermute | solution.py:36
  26.9 3.0 %grad_b_terms.1 = (f32[128,4096]{1,0:T(8,128)S(1)}, bf16[128,4096]{1,0:T(8,128)(2,1)S(1)}, bf16[1024,256]{1,0:T(8,128)(2,1)S(1)}) custom-call(s32[5]{0:T(128)S(1)} %stack.23.place, bf16[128,1024]{1,0:T(8,128)(2,1)S(1)} %pad_maximum_fusion.x0, bf16[128,1024]{1,0:T(8,128)(2,1)S(1)} %collective-permute-done.2.x1, bf16[1024,4096]{1,0:T(8,128)(2,1)S(1)} %get-tuple-element.15.g), custom_call_target="tpu_custom_call" | custom-call | flops 2147483648 | bytes 12582912 | tf_op jit(solution)/shard_map/grad_b_terms/pallas_call | solution.py:133
  30.9 2.8 %collective-permute-done.7.b3 = bf16[32,4096]{1,0:T(8,128)(2,1)S(1)} collective-permute-done((bf16[32,4096]{1,0:T(8,128)(2,1)S(1)}, bf16[32,4096]{1,0:T(8,128)(2,1)S(1)}, u32[]{:S(2)}, u32[]{:S(2)}) %collective-permute-start.7) | collective-permute-done | bytes 262176 | tf_op jit(solution)/shard_map/ppermute | solution.py:36
  35.2 2.4 %collective-permute-start.17 = (bf16[32,4096]{1,0:T(8,128)(2,1)S(1)}, bf16[32,4096]{1,0:T(8,128)(2,1)S(1)}, u32[]{:S(2)}, u32[]{:S(2)}) collective-permute-start(bf16[32,4096]{1,0:T(8,128)(2,1)S(1)} %get-tuple-element.28), channel_id=1, source_target_pairs={{0,32},{8,40},{16,48},{24,56},{32,0},{40,8},{48,16},{56,24},{64,96... | collective-permute-start | bytes 786440 | tf_op jit(solution)/shard_map/ppermute | solution.py:36
  37.6 1.2 %collective-permute-start.19 = (bf16[32,4096]{1,0:T(8,128)(2,1)S(1)}, bf16[32,4096]{1,0:T(8,128)(2,1)S(1)}, u32[]{:S(2)}, u32[]{:S(2)}) collective-permute-start(bf16[32,4096]{1,0:T(8,128)(2,1)S(1)} %get-tuple-element.30), channel_id=1, source_target_pairs={{0,16},{8,24},{16,32},{24,40},{32,48},{40,56},{48,0},{56,8},{64,80... | collective-permute-start | bytes 786440 | tf_op jit(solution)/shard_map/ppermute | solution.py:36
  38.9 2.0 %collective-permute-start.21 = (bf16[32,4096]{1,0:T(8,128)(2,1)S(1)}, bf16[32,4096]{1,0:T(8,128)(2,1)S(1)}, u32[]{:S(2)}, u32[]{:S(2)}) collective-permute-start(bf16[32,4096]{1,0:T(8,128)(2,1)S(1)} %get-tuple-element.29), channel_id=1, source_target_pairs={{0,48},{8,56},{16,0},{24,8},{32,16},{40,24},{48,32},{56,40},{64,11... | collective-permute-start | bytes 786440 | tf_op jit(solution)/shard_map/ppermute | solution.py:36
  40.9 3.0 %grad_a_terms.1 = (f32[128,1024]{1,0:T(8,128)S(1)}, bf16[128,1024]{1,0:T(8,128)(2,1)S(1)}, bf16[256,4096]{1,0:T(8,128)(2,1)S(1)}) custom-call(s32[5]{0:T(128)S(1)} %stack.23.place, bf16[32,4096]{1,0:T(8,128)(2,1)S(1)} %pad_maximum_fusion.1.b0, bf16[32,4096]{1,0:T(8,128)(2,1)S(1)} %collective-permute-done.5.b1, ...), custom_call_target="tpu_custom_call" | custom-call | flops 2147483648 | bytes 12582912 | tf_op jit(solution)/shard_map/grad_a_terms/pallas_call | solution.py:171
  43.9 1.6 %collective-permute-start.12 = (bf16[128,1024]{1,0:T(8,128)(2,1)S(1)}, bf16[128,1024]{1,0:T(8,128)(2,1)S(1)}, u32[]{:S(2)}, u32[]{:S(2)}) collective-permute-start(bf16[128,1024]{1,0:T(8,128)(2,1)S(1)} %get-tuple-element.20), channel_id=1, source_target_pairs={{0,6},{1,7},{2,4},{3,5},{4,2},{5,3},{6,0},{7,1},{8,14},{9,15},{10,... | collective-permute-start | bytes 786440 | tf_op jit(solution)/shard_map/ppermute | solution.py:44
  45.5 5.1 %pair_update.1 = bf16[32,128,128]{2,1,0:T(8,128)(2,1)} custom-call(bf16[1024,256]{1,0:T(8,128)(2,1)S(1)} %get-tuple-element.16.at, bf16[256,4096]{1,0:T(8,128)(2,1)S(1)} %get-tuple-element.17.b, bf16[128,1024]{1,0:T(8,128)(2,1)S(1)} %get-tuple-element.18.wt, f32[1,128]{1,0:T(1,128)S(1)} %bitcast.14), custom_call_target="tpu_custom_call" | custom-call | flops 3221225472 | bytes 4194304 | tf_op jit(solution)/shard_map/pair_update/pallas_call | solution.py:204
  50.5 1.1 %collective-permute-done.12 = bf16[128,1024]{1,0:T(8,128)(2,1)S(1)} collective-permute-done((bf16[128,1024]{1,0:T(8,128)(2,1)S(1)}, bf16[128,1024]{1,0:T(8,128)(2,1)S(1)}, u32[]{:S(2)}, u32[]{:S(2)}) %collective-permute-start.12) | collective-permute-done | bytes 262176 | tf_op jit(solution)/shard_map/ppermute | solution.py:44
  51.7 2.4 %collective-permute-start.13 = (bf16[64,1024]{1,0:T(8,128)(2,1)S(1)}, bf16[64,1024]{1,0:T(8,128)(2,1)S(1)}, u32[]{:S(2)}, u32[]{:S(2)}) collective-permute-start(bf16[64,1024]{1,0:T(8,128)(2,1)S(1)} %slice.100), channel_id=1, source_target_pairs={{0,2},{1,3},{2,0},{3,1},{4,6},{5,7},{6,4},{7,5},{8,10},{9,11},{10,... | collective-permute-start | bytes 393224 | tf_op jit(solution)/shard_map/ppermute | solution.py:44
  54.4 3.6 %collective-permute-start.22 = (bf16[8,4096]{1,0:T(8,128)(2,1)S(1)}, bf16[8,4096]{1,0:T(8,128)(2,1)S(1)}, u32[]{:S(2)}, u32[]{:S(2)}) collective-permute-start(bf16[8,4096]{1,0:T(8,128)(2,1)S(1)} %get-tuple-element.35), channel_id=1, source_target_pairs={{0,128},{8,136},{16,144},{24,152},{32,160},{40,168},{48,176},{56,1... | collective-permute-start | bytes 196616 | tf_op jit(solution)/shard_map/ppermute | solution.py:32
  57.9 2.6 %collective-permute-start.23 = (bf16[8,4096]{1,0:T(8,128)(2,1)S(1)}, bf16[8,4096]{1,0:T(8,128)(2,1)S(1)}, u32[]{:S(2)}, u32[]{:S(2)}) collective-permute-start(bf16[8,4096]{1,0:T(8,128)(2,1)S(1)} %get-tuple-element.37), channel_id=1, source_target_pairs={{0,64},{8,72},{16,80},{24,88},{32,96},{40,104},{48,112},{56,120},{... | collective-permute-start | bytes 196616 | tf_op jit(solution)/shard_map/ppermute | solution.py:32
  61.4 3.0 %collective-permute-start.14 = (bf16[32,1024]{1,0:T(8,128)(2,1)S(1)}, bf16[32,1024]{1,0:T(8,128)(2,1)S(1)}, u32[]{:S(2)}, u32[]{:S(2)}) collective-permute-start(bf16[32,1024]{1,0:T(8,128)(2,1)S(1)} %slice.101), channel_id=1, source_target_pairs={{0,1},{1,0},{2,3},{3,2},{4,5},{5,4},{6,7},{7,6},{8,9},{9,8},{10,11... | collective-permute-start | bytes 196616 | tf_op jit(solution)/shard_map/ppermute | solution.py:48
  64.5 2.5 %collective-permute-done.24 = bf16[8,4096]{1,0:T(8,128)(2,1)S(1)} collective-permute-done((bf16[8,4096]{1,0:T(8,128)(2,1)S(1)}, bf16[8,4096]{1,0:T(8,128)(2,1)S(1)}, u32[]{:S(2)}, u32[]{:S(2)}) %collective-permute-start.24) | collective-permute-done | bytes 65568 | tf_op jit(solution)/shard_map/ppermute | solution.py:32
  (53 shorter events, 7.1 us)
Async XLA Ops:
  2.0 6.3 %collective-permute-start = (bf16[32,1024]{1,0:T(8,128)(2,1)S(1)}, bf16[32,1024]{1,0:T(8,128)(2,1)S(1)}, u32[]{:S(2)}, u32[]{:S(2)}) collective-permute-start(bf16[32,1024]{1,0:T(8,128)(2,1)S(1)} %reshape.21), channel_id=1, source_target_pairs={{0,1},{1,0},{2,3},{3,2},{4,5},{5,4},{6,7},{7,6},{8,9},{9,8},{10,11... | collective-permute-start | bytes 196616 | tf_op jit(solution)/shard_map/ppermute | solution.py:48
  4.9 6.4 %collective-permute-start.3 = (bf16[8,4096]{1,0:T(8,128)(2,1)S(1)}, bf16[8,4096]{1,0:T(8,128)(2,1)S(1)}, u32[]{:S(2)}, u32[]{:S(2)}) collective-permute-start(bf16[8,4096]{1,0:T(8,128)(2,1)S(1)} %bitcast.15), channel_id=1, source_target_pairs={{0,64},{8,72},{16,80},{24,88},{32,96},{40,104},{48,112},{56,120},{... | collective-permute-start | bytes 196616 | tf_op jit(solution)/shard_map/ppermute | solution.py:32
  8.4 11.4 %collective-permute-start.1 = (bf16[64,1024]{1,0:T(8,128)(2,1)S(1)}, bf16[64,1024]{1,0:T(8,128)(2,1)S(1)}, u32[]{:S(2)}, u32[]{:S(2)}) collective-permute-start(bf16[64,1024]{1,0:T(8,128)(2,1)S(1)} %pad_maximum_fusion.2), channel_id=1, source_target_pairs={{0,2},{1,3},{2,0},{3,1},{4,6},{5,7},{6,4},{7,5},{8,10},{9,11},{10,... | collective-permute-start | bytes 393224 | tf_op jit(solution)/shard_map/ppermute | solution.py:44
  11.4 9.0 %collective-permute-start.4 = (bf16[16,4096]{1,0:T(8,128)(2,1)S(1)}, bf16[16,4096]{1,0:T(8,128)(2,1)S(1)}, u32[]{:S(2)}, u32[]{:S(2)}) collective-permute-start(bf16[16,4096]{1,0:T(8,128)(2,1)S(1)} %pad_maximum_fusion.3), channel_id=1, source_target_pairs={{0,192},{8,200},{16,208},{24,216},{32,224},{40,232},{48,240},{56,2... | collective-permute-start | bytes 393224 | tf_op jit(solution)/shard_map/ppermute | solution.py:32
  19.8 7.2 %collective-permute-start.2 = (bf16[128,1024]{1,0:T(8,128)(2,1)S(1)}, bf16[128,1024]{1,0:T(8,128)(2,1)S(1)}, u32[]{:S(2)}, u32[]{:S(2)}) collective-permute-start(bf16[128,1024]{1,0:T(8,128)(2,1)S(1)} %pad_maximum_fusion.x0), channel_id=1, source_target_pairs={{0,6},{1,7},{2,4},{3,5},{4,2},{5,3},{6,0},{7,1},{8,14},{9,15},{10,... | collective-permute-start | bytes 786440 | tf_op jit(solution)/shard_map/ppermute | solution.py:44
  20.4 10.5 %collective-permute-start.6 = (bf16[32,4096]{1,0:T(8,128)(2,1)S(1)}, bf16[32,4096]{1,0:T(8,128)(2,1)S(1)}, u32[]{:S(2)}, u32[]{:S(2)}) collective-permute-start(bf16[32,4096]{1,0:T(8,128)(2,1)S(1)} %pad_maximum_fusion.1.b0), channel_id=1, source_target_pairs={{0,32},{8,40},{16,48},{24,56},{32,0},{40,8},{48,16},{56,24},{64,96... | collective-permute-start | bytes 786440 | tf_op jit(solution)/shard_map/ppermute | solution.py:36
  23.7 10.0 %collective-permute-start.7 = (bf16[32,4096]{1,0:T(8,128)(2,1)S(1)}, bf16[32,4096]{1,0:T(8,128)(2,1)S(1)}, u32[]{:S(2)}, u32[]{:S(2)}) collective-permute-start(bf16[32,4096]{1,0:T(8,128)(2,1)S(1)} %pad_maximum_fusion.1.b0), channel_id=1, source_target_pairs={{0,16},{8,24},{16,32},{24,40},{32,48},{40,56},{48,0},{56,8},{64,80... | collective-permute-start | bytes 786440 | tf_op jit(solution)/shard_map/ppermute | solution.py:36
  24.4 9.6 %collective-permute-start.5 = (bf16[32,4096]{1,0:T(8,128)(2,1)S(1)}, bf16[32,4096]{1,0:T(8,128)(2,1)S(1)}, u32[]{:S(2)}, u32[]{:S(2)}) collective-permute-start(bf16[32,4096]{1,0:T(8,128)(2,1)S(1)} %pad_maximum_fusion.1.b0), channel_id=1, source_target_pairs={{0,48},{8,56},{16,0},{24,8},{32,16},{40,24},{48,32},{56,40},{64,11... | collective-permute-start | bytes 786440 | tf_op jit(solution)/shard_map/ppermute | solution.py:36
  30.0 4.2 %collective-permute-start.16 = (bf16[32,4096]{1,0:T(8,128)(2,1)S(1)}, bf16[32,4096]{1,0:T(8,128)(2,1)S(1)}, u32[]{:S(2)}, u32[]{:S(2)}) collective-permute-start(bf16[32,4096]{1,0:T(8,128)(2,1)S(1)} %get-tuple-element.34), channel_id=1, source_target_pairs={{0,8},{8,0},{16,24},{24,16},{32,40},{40,32},{48,56},{56,48},{64,72... | collective-permute-start | bytes 786440 | tf_op jit(solution)/shard_map/ppermute | solution.py:40
  30.1 4.4 %collective-permute-start.18 = (bf16[32,4096]{1,0:T(8,128)(2,1)S(1)}, bf16[32,4096]{1,0:T(8,128)(2,1)S(1)}, u32[]{:S(2)}, u32[]{:S(2)}) collective-permute-start(bf16[32,4096]{1,0:T(8,128)(2,1)S(1)} %get-tuple-element.33), channel_id=1, source_target_pairs={{0,8},{8,0},{16,24},{24,16},{32,40},{40,32},{48,56},{56,48},{64,72... | collective-permute-start | bytes 786440 | tf_op jit(solution)/shard_map/ppermute | solution.py:40
  30.9 3.8 %collective-permute-start.20 = (bf16[32,4096]{1,0:T(8,128)(2,1)S(1)}, bf16[32,4096]{1,0:T(8,128)(2,1)S(1)}, u32[]{:S(2)}, u32[]{:S(2)}) collective-permute-start(bf16[32,4096]{1,0:T(8,128)(2,1)S(1)} %get-tuple-element.32), channel_id=1, source_target_pairs={{0,8},{8,0},{16,24},{24,16},{32,40},{40,32},{48,56},{56,48},{64,72... | collective-permute-start | bytes 786440 | tf_op jit(solution)/shard_map/ppermute | solution.py:40
  34.0 20.1 %collective-permute-start.15 = (bf16[32,4096]{1,0:T(8,128)(2,1)S(1)}, bf16[32,4096]{1,0:T(8,128)(2,1)S(1)}, u32[]{:S(2)}, u32[]{:S(2)}) collective-permute-start(bf16[32,4096]{1,0:T(8,128)(2,1)S(1)} %get-tuple-element.31), channel_id=1, source_target_pairs={{0,8},{8,0},{16,24},{24,16},{32,40},{40,32},{48,56},{56,48},{64,72... | collective-permute-start | bytes 786440 | tf_op jit(solution)/shard_map/ppermute | solution.py:40
  34.2 3.4 %collective-permute-start.10 = (bf16[32,4096]{1,0:T(8,128)(2,1)S(1)}, bf16[32,4096]{1,0:T(8,128)(2,1)S(1)}, u32[]{:S(2)}, u32[]{:S(2)}) collective-permute-start(bf16[32,4096]{1,0:T(8,128)(2,1)S(1)} %collective-permute-done.6.b2), channel_id=1, source_target_pairs={{0,8},{8,0},{16,24},{24,16},{32,40},{40,32},{48,56},{56,48},{64,72... | collective-permute-start | bytes 786440 | tf_op jit(solution)/shard_map/ppermute | solution.py:40
  34.5 4.3 %collective-permute-start.11 = (bf16[32,4096]{1,0:T(8,128)(2,1)S(1)}, bf16[32,4096]{1,0:T(8,128)(2,1)S(1)}, u32[]{:S(2)}, u32[]{:S(2)}) collective-permute-start(bf16[32,4096]{1,0:T(8,128)(2,1)S(1)} %collective-permute-done.7.b3), channel_id=1, source_target_pairs={{0,8},{8,0},{16,24},{24,16},{32,40},{40,32},{48,56},{56,48},{64,72... | collective-permute-start | bytes 786440 | tf_op jit(solution)/shard_map/ppermute | solution.py:40
  34.7 6.2 %collective-permute-start.9 = (bf16[32,4096]{1,0:T(8,128)(2,1)S(1)}, bf16[32,4096]{1,0:T(8,128)(2,1)S(1)}, u32[]{:S(2)}, u32[]{:S(2)}) collective-permute-start(bf16[32,4096]{1,0:T(8,128)(2,1)S(1)} %collective-permute-done.5.b1), channel_id=1, source_target_pairs={{0,8},{8,0},{16,24},{24,16},{32,40},{40,32},{48,56},{56,48},{64,72... | collective-permute-start | bytes 786440 | tf_op jit(solution)/shard_map/ppermute | solution.py:40
  35.2 18.9 %collective-permute-start.17 = (bf16[32,4096]{1,0:T(8,128)(2,1)S(1)}, bf16[32,4096]{1,0:T(8,128)(2,1)S(1)}, u32[]{:S(2)}, u32[]{:S(2)}) collective-permute-start(bf16[32,4096]{1,0:T(8,128)(2,1)S(1)} %get-tuple-element.28), channel_id=1, source_target_pairs={{0,32},{8,40},{16,48},{24,56},{32,0},{40,8},{48,16},{56,24},{64,96... | collective-permute-start | bytes 786440 | tf_op jit(solution)/shard_map/ppermute | solution.py:36
  37.6 16.5 %collective-permute-start.19 = (bf16[32,4096]{1,0:T(8,128)(2,1)S(1)}, bf16[32,4096]{1,0:T(8,128)(2,1)S(1)}, u32[]{:S(2)}, u32[]{:S(2)}) collective-permute-start(bf16[32,4096]{1,0:T(8,128)(2,1)S(1)} %get-tuple-element.30), channel_id=1, source_target_pairs={{0,16},{8,24},{16,32},{24,40},{32,48},{40,56},{48,0},{56,8},{64,80... | collective-permute-start | bytes 786440 | tf_op jit(solution)/shard_map/ppermute | solution.py:36
  38.9 15.3 %collective-permute-start.21 = (bf16[32,4096]{1,0:T(8,128)(2,1)S(1)}, bf16[32,4096]{1,0:T(8,128)(2,1)S(1)}, u32[]{:S(2)}, u32[]{:S(2)}) collective-permute-start(bf16[32,4096]{1,0:T(8,128)(2,1)S(1)} %get-tuple-element.29), channel_id=1, source_target_pairs={{0,48},{8,56},{16,0},{24,8},{32,16},{40,24},{48,32},{56,40},{64,11... | collective-permute-start | bytes 786440 | tf_op jit(solution)/shard_map/ppermute | solution.py:36
  43.9 7.7 %collective-permute-start.12 = (bf16[128,1024]{1,0:T(8,128)(2,1)S(1)}, bf16[128,1024]{1,0:T(8,128)(2,1)S(1)}, u32[]{:S(2)}, u32[]{:S(2)}) collective-permute-start(bf16[128,1024]{1,0:T(8,128)(2,1)S(1)} %get-tuple-element.20), channel_id=1, source_target_pairs={{0,6},{1,7},{2,4},{3,5},{4,2},{5,3},{6,0},{7,1},{8,14},{9,15},{10,... | collective-permute-start | bytes 786440 | tf_op jit(solution)/shard_map/ppermute | solution.py:44
  51.7 9.7 %collective-permute-start.13 = (bf16[64,1024]{1,0:T(8,128)(2,1)S(1)}, bf16[64,1024]{1,0:T(8,128)(2,1)S(1)}, u32[]{:S(2)}, u32[]{:S(2)}) collective-permute-start(bf16[64,1024]{1,0:T(8,128)(2,1)S(1)} %slice.100), channel_id=1, source_target_pairs={{0,2},{1,3},{2,0},{3,1},{4,6},{5,7},{6,4},{7,5},{8,10},{9,11},{10,... | collective-permute-start | bytes 393224 | tf_op jit(solution)/shard_map/ppermute | solution.py:44
  54.4 10.1 %collective-permute-start.22 = (bf16[8,4096]{1,0:T(8,128)(2,1)S(1)}, bf16[8,4096]{1,0:T(8,128)(2,1)S(1)}, u32[]{:S(2)}, u32[]{:S(2)}) collective-permute-start(bf16[8,4096]{1,0:T(8,128)(2,1)S(1)} %get-tuple-element.35), channel_id=1, source_target_pairs={{0,128},{8,136},{16,144},{24,152},{32,160},{40,168},{48,176},{56,1... | collective-permute-start | bytes 196616 | tf_op jit(solution)/shard_map/ppermute | solution.py:32
  57.9 6.5 %collective-permute-start.23 = (bf16[8,4096]{1,0:T(8,128)(2,1)S(1)}, bf16[8,4096]{1,0:T(8,128)(2,1)S(1)}, u32[]{:S(2)}, u32[]{:S(2)}) collective-permute-start(bf16[8,4096]{1,0:T(8,128)(2,1)S(1)} %get-tuple-element.37), channel_id=1, source_target_pairs={{0,64},{8,72},{16,80},{24,88},{32,96},{40,104},{48,112},{56,120},{... | collective-permute-start | bytes 196616 | tf_op jit(solution)/shard_map/ppermute | solution.py:32
  60.6 6.4 %collective-permute-start.24 = (bf16[8,4096]{1,0:T(8,128)(2,1)S(1)}, bf16[8,4096]{1,0:T(8,128)(2,1)S(1)}, u32[]{:S(2)}, u32[]{:S(2)}) collective-permute-start(bf16[8,4096]{1,0:T(8,128)(2,1)S(1)} %get-tuple-element.36), channel_id=1, source_target_pairs={{0,192},{8,200},{16,208},{24,216},{32,224},{40,232},{48,240},{56,2... | collective-permute-start | bytes 196616 | tf_op jit(solution)/shard_map/ppermute | solution.py:32
  61.4 6.2 %collective-permute-start.14 = (bf16[32,1024]{1,0:T(8,128)(2,1)S(1)}, bf16[32,1024]{1,0:T(8,128)(2,1)S(1)}, u32[]{:S(2)}, u32[]{:S(2)}) collective-permute-start(bf16[32,1024]{1,0:T(8,128)(2,1)S(1)} %slice.101), channel_id=1, source_target_pairs={{0,1},{1,0},{2,3},{3,2},{4,5},{5,4},{6,7},{7,6},{8,9},{9,8},{10,11... | collective-permute-start | bytes 196616 | tf_op jit(solution)/shard_map/ppermute | solution.py:48
  (2 other events, 8.1 us)

commit v3 on v2

--- a/solution.py
+++ b/solution.py
@@ -20,12 +20,23 @@
     perm = []
     for w in range(32):
         z, y, c = w // 8, (w // 2) % 4, w % 2
-        perm.append((w, ((z ^ dz) * 4 + (y + dy) % 4) * 2 + (c ^ dc)))
+        perm.append((w, ((z ^ dz[c]) * 4 + (y + dy) % 4) * 2 + (c ^ dc)))
     return perm
 
 
-def narrow_perm(dx, dl):
-    return [(n, ((n // 2) ^ dx) * 2 + ((n % 2) ^ dl)) for n in range(8)]
+def narrow_perm(dl):
+    return [(n, n ^ dl) for n in range(8)]
+
+
+FIRST, SECOND = (1, 3), (3, 1)
+
+
+def x_perm(d):
+    perm = []
+    for w in range(32):
+        for n in range(8):
+            perm.append((w * 8 + n, w * 8 + ((n // 2) ^ d[w % 2]) * 2 + n % 2))
+    return perm
 
 
 def swap_z(v, d):
@@ -33,19 +44,19 @@
 
 
 def send_y(v, k):
-    return lax.ppermute(v, "wide", wide_perm(0, k, 0))
+    return lax.ppermute(v, "wide", wide_perm((0, 0), k, 0))
 
 
 def swap_core(v):
-    return lax.ppermute(v, "wide", wide_perm(0, 0, 1))
+    return lax.ppermute(v, "wide", wide_perm((0, 0), 0, 1))
 
 
 def swap_x(v, d):
-    return lax.ppermute(v, "narrow", narrow_perm(d, 0))
+    return lax.ppermute(v, ("wide", "narrow"), x_perm(d))
 
 
 def swap_l(v):
-    return lax.ppermute(v, "narrow", narrow_perm(0, 1))
+    return lax.ppermute(v, "narrow", narrow_perm(1))
 
 
 def both(v, w):
@@ -54,7 +65,9 @@
 
 def own_row(place, qx, rl, yl, core):
     z, y, c, x, l = (place[q] for q in range(5))
-    d = (x ^ (0, 1, 3, 2)[qx]) ^ z
+    on0, on1 = (0, 1, 3, 2)[qx], (0, 3, 1, 2)[qx]
+    d = (x ^ (on0 + c * (on1 - on0))) ^ z
+    d = d ^ ((d & 1) * 2 * core)
     zz = d ^ (d >> 1)
     yy = lax.rem(2 * (l ^ rl) + yl - y + 4, 4)
     cc = core ^ c
@@ -225,14 +238,14 @@
     place = jnp.stack([w >> 3, (w >> 1) & 3, w & 1, n >> 1, n & 1]).astype(jnp.int32)
 
     b0 = lax.optimization_barrier(proj_b.reshape(8, C * COLS))
-    b1 = both(b0, swap_z(b0, 1))
+    b1 = both(b0, swap_z(b0, FIRST))
 
     a0 = lax.optimization_barrier(proj_a.transpose(0, 2, 1).reshape(32, ROWS * C))
     a1 = both(a0, swap_l(a0))
-    a2 = both(a1, swap_x(a1, 1))
-    xs = [a2, swap_x(a2, 3)]
-
-    b2 = both(b1, swap_z(b1, 3))
+    a2 = both(a1, swap_x(a1, FIRST))
+    xs = [a2, swap_x(a2, SECOND)]
+
+    b2 = both(b1, swap_z(b1, SECOND))
     ys = [b2] + [send_y(b2, -k) for k in (1, 2, 3)]
     bs = ys + [swap_core(v) for v in ys]
 
@@ -248,13 +261,13 @@
     for k in (2, 1, 3):
         total = total + send_y(parts[k].astype(BF16), k).astype(F32)
     b_summed = total[:8]
-    for q, d in ((3, 2), (1, 1), (2, 3)):
+    for q, d in ((3, (2, 2)), (1, FIRST), (2, SECOND)):
         b_summed = b_summed + swap_z(total[8 * q:8 * (q + 1)].astype(BF16), d).astype(F32)
     grad_b = (b_summed * SCALE).astype(BF16).reshape(8, C, COLS)
 
     keep, away, b_full = grad_a_terms(place, bs, g)
-    total = keep + swap_x(away, 3).astype(F32)
-    total = total[:64] + swap_x(total[64:].astype(BF16), 1).astype(F32)
+    total = keep + swap_x(away, SECOND).astype(F32)
+    total = total[:64] + swap_x(total[64:].astype(BF16), FIRST).astype(F32)
     a_summed = total[:32] + swap_l(total[32:].astype(BF16)).astype(F32)
     grad_a = (a_summed * SCALE).astype(BF16).reshape(32, ROWS, C).transpose(0, 2, 1)
 

time: 68.9 us -> 67.7 us (0.983)
  the two profiles are of different devices: /device:TPU:4 before, /device:TPU:1 now
where the time goes in v3:
time: 67.7 us; the launch traced here: 66.4 us
  starting transfers between devices  40.8 us (60%)
  Pallas kernels  15 us (22%)
  waiting for transfers between devices  5.08 us (8%)
  local copies, waits for them, and re-layouts  4.14 us (6%)
  between operations  0.8 us (1%)
    ppermute x5, starting transfers between devices, swap_z(): return lax.ppermute(v, 'wide', wide_perm(d, 0, 0))  12.2 us
    ppermute x6, starting transfers between devices, send_y(): return lax.ppermute(v, 'wide', wide_perm((0, 0), k, 0))  10.6 us
    ppermute x8, starting transfers between devices, swap_core(): return lax.ppermute(v, 'wide', wide_perm((0, 0), 0, 1))  8.16 us
    ppermute x4, starting transfers between devices, swap_x(): return lax.ppermute(v, ('wide', 'narrow'), x_perm(d))  6.72 us
    pallas_call x1, Pallas kernels, pair_update(): pl.pallas_call(update_kernel, grid=(ROWS // step,), in_specs=[pl.BlockSpe...  5.06 us
    ppermute x5, waiting for transfers between devices, swap_z(): return lax.ppermute(v, 'wide', wide_perm(d, 0, 0))  5.03 us
    pallas_call x1, Pallas kernels, grad_outer(): pl.pallas_call(grad_outer_kernel, grid=(ROWS // step,), in_specs=[pl.Bloc...  3.97 us
    ppermute x2, starting transfers between devices, swap_l(): return lax.ppermute(v, 'narrow', narrow_perm(1))  3.11 us
  transfers between devices with their start and end apart: 25, of which 3 were waited for; matrix products, arithmetic and copies ran while one was open for 3% of the time, Pallas kernels for 23%

profile of v3, /device:TPU:1, one launch (start us, length us, event | category | flops | bytes accessed | tf_op | source)
XLA Modules:
  0.0 66.4 jit_solution(4065757823034132992)
XLA Ops:
  0.6 1.1 %copy.8 = bf16[32,32,32]{2,1,0:T(8,128)(2,1)S(1)} copy(bf16[32,32,32]{1,2,0:T(8,128)(2,1)} %bitcast.18) | data formatting | bytes 131072 | tf_op jit(solution)/shard_map/transpose | solution.py:243
  2.0 2.6 %collective-permute-start = (bf16[32,1024]{1,0:T(8,128)(2,1)S(1)}, bf16[32,1024]{1,0:T(8,128)(2,1)S(1)}, u32[]{:S(2)}, u32[]{:S(2)}) collective-permute-start(bf16[32,1024]{1,0:T(8,128)(2,1)S(1)} %reshape.21), channel_id=1, source_target_pairs={{0,1},{1,0},{2,3},{3,2},{4,5},{5,4},{6,7},{7,6},{8,9},{9,8},{10,11... | collective-permute-start | bytes 196616 | tf_op jit(solution)/shard_map/ppermute | solution.py:59
  4.6 0.9 %copy.13 = bf16[1,8,32,128]{3,1,2,0:T(8,128)(2,1)S(1)} copy(bf16[1,8,32,128]{3,2,1,0:T(8,128)(2,1)} %bitcast.20) | data formatting | bytes 131072
  5.4 5.2 %collective-permute-start.3 = (bf16[8,4096]{1,0:T(8,128)(2,1)S(1)}, bf16[8,4096]{1,0:T(8,128)(2,1)S(1)}, u32[]{:S(2)}, u32[]{:S(2)}) collective-permute-start(bf16[8,4096]{1,0:T(8,128)(2,1)S(1)} %bitcast.15), channel_id=1, source_target_pairs={{0,64},{8,200},{16,80},{24,216},{32,96},{40,232},{48,112},{56,248}... | collective-permute-start | bytes 196616 | tf_op jit(solution)/shard_map/ppermute | solution.py:43
  10.8 2.6 %collective-permute-start.1 = (bf16[64,1024]{1,0:T(8,128)(2,1)S(1)}, bf16[64,1024]{1,0:T(8,128)(2,1)S(1)}, u32[]{:S(2)}, u32[]{:S(2)}) collective-permute-start(bf16[64,1024]{1,0:T(8,128)(2,1)S(1)} %pad_maximum_fusion.2), channel_id=1, source_target_pairs={{0,2},{1,3},{2,0},{3,1},{4,6},{5,7},{6,4},{7,5},{8,14},{9,15},{10,... | collective-permute-start | bytes 393224 | tf_op jit(solution)/shard_map/ppermute | solution.py:55
  13.3 1.3 %collective-permute-start.4 = (bf16[16,4096]{1,0:T(8,128)(2,1)S(1)}, bf16[16,4096]{1,0:T(8,128)(2,1)S(1)}, u32[]{:S(2)}, u32[]{:S(2)}) collective-permute-start(bf16[16,4096]{1,0:T(8,128)(2,1)S(1)} %pad_maximum_fusion.3), channel_id=1, source_target_pairs={{0,192},{8,72},{16,208},{24,88},{32,224},{40,104},{48,240},{56,120... | collective-permute-start | bytes 393224 | tf_op jit(solution)/shard_map/ppermute | solution.py:43
  14.6 4.0 %grad_outer.1 = (bf16[1024,4096]{1,0:T(8,128)(2,1)S(1)}, bf16[128,1024]{1,0:T(8,128)(2,1)S(1)}) custom-call(bf16[32,128,128]{2,1,0:T(8,128)(2,1)} %cot, bf16[1024,128]{1,0:T(8,128)(2,1)} %w.1), custom_call_target="tpu_custom_call" | custom-call | flops 1073741824 | bytes 9437184 | tf_op jit(solution)/shard_map/grad_outer/pallas_call | solution.py:96
  18.6 1.2 %collective-permute-start.2 = (bf16[128,1024]{1,0:T(8,128)(2,1)S(1)}, bf16[128,1024]{1,0:T(8,128)(2,1)S(1)}, u32[]{:S(2)}, u32[]{:S(2)}) collective-permute-start(bf16[128,1024]{1,0:T(8,128)(2,1)S(1)} %pad_maximum_fusion.x0), channel_id=1, source_target_pairs={{0,6},{1,7},{2,4},{3,5},{4,2},{5,3},{6,0},{7,1},{8,10},{9,11},{10,... | collective-permute-start | bytes 786440 | tf_op jit(solution)/shard_map/ppermute | solution.py:55
  19.9 3.0 %collective-permute-start.6 = (bf16[32,4096]{1,0:T(8,128)(2,1)S(1)}, bf16[32,4096]{1,0:T(8,128)(2,1)S(1)}, u32[]{:S(2)}, u32[]{:S(2)}) collective-permute-start(bf16[32,4096]{1,0:T(8,128)(2,1)S(1)} %pad_maximum_fusion.1.b0), channel_id=1, source_target_pairs={{0,32},{8,40},{16,48},{24,56},{32,0},{40,8},{48,16},{56,24},{64,96... | collective-permute-start | bytes 786440 | tf_op jit(solution)/shard_map/ppermute | solution.py:47
  23.3 2.3 %collective-permute-start.5 = (bf16[32,4096]{1,0:T(8,128)(2,1)S(1)}, bf16[32,4096]{1,0:T(8,128)(2,1)S(1)}, u32[]{:S(2)}, u32[]{:S(2)}) collective-permute-start(bf16[32,4096]{1,0:T(8,128)(2,1)S(1)} %pad_maximum_fusion.1.b0), channel_id=1, source_target_pairs={{0,48},{8,56},{16,0},{24,8},{32,16},{40,24},{48,32},{56,40},{64,11... | collective-permute-start | bytes 786440 | tf_op jit(solution)/shard_map/ppermute | solution.py:47
  25.6 3.0 %grad_b_terms.1 = (f32[128,4096]{1,0:T(8,128)S(1)}, bf16[128,4096]{1,0:T(8,128)(2,1)S(1)}, bf16[1024,256]{1,0:T(8,128)(2,1)S(1)}) custom-call(s32[5]{0:T(128)S(1)} %stack.23.place, bf16[128,1024]{1,0:T(8,128)(2,1)S(1)} %pad_maximum_fusion.x0, bf16[128,1024]{1,0:T(8,128)(2,1)S(1)} %collective-permute-done.2.x1, bf16[1024,4096]{1,0:T(8,128)(2,1)S(1)} %get-tuple-element.15.g), custom_call_target="tpu_custom_call" | custom-call | flops 2147483648 | bytes 12582912 | tf_op jit(solution)/shard_map/grad_b_terms/pallas_call | solution.py:146
  28.7 5.6 %collective-permute-start.16 = (bf16[32,4096]{1,0:T(8,128)(2,1)S(1)}, bf16[32,4096]{1,0:T(8,128)(2,1)S(1)}, u32[]{:S(2)}, u32[]{:S(2)}) collective-permute-start(bf16[32,4096]{1,0:T(8,128)(2,1)S(1)} %get-tuple-element.34), channel_id=1, source_target_pairs={{0,8},{8,0},{16,24},{24,16},{32,40},{40,32},{48,56},{56,48},{64,72... | collective-permute-start | bytes 786440 | tf_op jit(solution)/shard_map/ppermute | solution.py:51
  34.8 1.0 %collective-permute-start.8 = (bf16[32,4096]{1,0:T(8,128)(2,1)S(1)}, bf16[32,4096]{1,0:T(8,128)(2,1)S(1)}, u32[]{:S(2)}, u32[]{:S(2)}) collective-permute-start(bf16[32,4096]{1,0:T(8,128)(2,1)S(1)} %pad_maximum_fusion.1.b0), channel_id=1, source_target_pairs={{0,8},{8,0},{16,24},{24,16},{32,40},{40,32},{48,56},{56,48},{64,72... | collective-permute-start | bytes 786440 | tf_op jit(solution)/shard_map/ppermute | solution.py:51
  37.1 2.2 %collective-permute-start.17 = (bf16[32,4096]{1,0:T(8,128)(2,1)S(1)}, bf16[32,4096]{1,0:T(8,128)(2,1)S(1)}, u32[]{:S(2)}, u32[]{:S(2)}) collective-permute-start(bf16[32,4096]{1,0:T(8,128)(2,1)S(1)} %get-tuple-element.28), channel_id=1, source_target_pairs={{0,32},{8,40},{16,48},{24,56},{32,0},{40,8},{48,16},{56,24},{64,96... | collective-permute-start | bytes 786440 | tf_op jit(solution)/shard_map/ppermute | solution.py:47
  40.0 1.9 %collective-permute-start.21 = (bf16[32,4096]{1,0:T(8,128)(2,1)S(1)}, bf16[32,4096]{1,0:T(8,128)(2,1)S(1)}, u32[]{:S(2)}, u32[]{:S(2)}) collective-permute-start(bf16[32,4096]{1,0:T(8,128)(2,1)S(1)} %get-tuple-element.29), channel_id=1, source_target_pairs={{0,48},{8,56},{16,0},{24,8},{32,16},{40,24},{48,32},{56,40},{64,11... | collective-permute-start | bytes 786440 | tf_op jit(solution)/shard_map/ppermute | solution.py:47
  42.0 3.0 %grad_a_terms.1 = (f32[128,1024]{1,0:T(8,128)S(1)}, bf16[128,1024]{1,0:T(8,128)(2,1)S(1)}, bf16[256,4096]{1,0:T(8,128)(2,1)S(1)}) custom-call(s32[5]{0:T(128)S(1)} %stack.23.place, bf16[32,4096]{1,0:T(8,128)(2,1)S(1)} %pad_maximum_fusion.1.b0, bf16[32,4096]{1,0:T(8,128)(2,1)S(1)} %collective-permute-done.5.b1, ...), custom_call_target="tpu_custom_call" | custom-call | flops 2147483648 | bytes 12582912 | tf_op jit(solution)/shard_map/grad_a_terms/pallas_call | solution.py:184
  45.7 5.1 %pair_update.1 = bf16[32,128,128]{2,1,0:T(8,128)(2,1)} custom-call(bf16[1024,256]{1,0:T(8,128)(2,1)S(1)} %get-tuple-element.16.at, bf16[256,4096]{1,0:T(8,128)(2,1)S(1)} %get-tuple-element.17.b, bf16[128,1024]{1,0:T(8,128)(2,1)S(1)} %get-tuple-element.18.wt, f32[1,128]{1,0:T(1,128)S(1)} %bitcast.14), custom_call_target="tpu_custom_call" | custom-call | flops 3221225472 | bytes 4194304 | tf_op jit(solution)/shard_map/pair_update/pallas_call | solution.py:217
  50.9 2.1 %collective-permute-start.13 = (bf16[64,1024]{1,0:T(8,128)(2,1)S(1)}, bf16[64,1024]{1,0:T(8,128)(2,1)S(1)}, u32[]{:S(2)}, u32[]{:S(2)}) collective-permute-start(bf16[64,1024]{1,0:T(8,128)(2,1)S(1)} %slice.100), channel_id=1, source_target_pairs={{0,2},{1,3},{2,0},{3,1},{4,6},{5,7},{6,4},{7,5},{8,14},{9,15},{10,... | collective-permute-start | bytes 393224 | tf_op jit(solution)/shard_map/ppermute | solution.py:55
  53.2 4.3 %collective-permute-start.22 = (bf16[8,4096]{1,0:T(8,128)(2,1)S(1)}, bf16[8,4096]{1,0:T(8,128)(2,1)S(1)}, u32[]{:S(2)}, u32[]{:S(2)}) collective-permute-start(bf16[8,4096]{1,0:T(8,128)(2,1)S(1)} %get-tuple-element.35), channel_id=1, source_target_pairs={{0,128},{8,136},{16,144},{24,152},{32,160},{40,168},{48,176},{56,1... | collective-permute-start | bytes 196616 | tf_op jit(solution)/shard_map/ppermute | solution.py:43
  57.5 1.4 %collective-permute-start.24 = (bf16[8,4096]{1,0:T(8,128)(2,1)S(1)}, bf16[8,4096]{1,0:T(8,128)(2,1)S(1)}, u32[]{:S(2)}, u32[]{:S(2)}) collective-permute-start(bf16[8,4096]{1,0:T(8,128)(2,1)S(1)} %get-tuple-element.36), channel_id=1, source_target_pairs={{0,192},{8,72},{16,208},{24,88},{32,224},{40,104},{48,240},{56,120... | collective-permute-start | bytes 196616 | tf_op jit(solution)/shard_map/ppermute | solution.py:43
  59.6 0.8 %collective-permute-done.22 = bf16[8,4096]{1,0:T(8,128)(2,1)S(1)} collective-permute-done((bf16[8,4096]{1,0:T(8,128)(2,1)S(1)}, bf16[8,4096]{1,0:T(8,128)(2,1)S(1)}, u32[]{:S(2)}, u32[]{:S(2)}) %collective-permute-start.22) | collective-permute-done | bytes 65568 | tf_op jit(solution)/shard_map/ppermute | solution.py:43
  60.4 2.5 %collective-permute-done.23 = bf16[8,4096]{1,0:T(8,128)(2,1)S(1)} collective-permute-done((bf16[8,4096]{1,0:T(8,128)(2,1)S(1)}, bf16[8,4096]{1,0:T(8,128)(2,1)S(1)}, u32[]{:S(2)}, u32[]{:S(2)}) %collective-permute-start.23) | collective-permute-done | bytes 65568 | tf_op jit(solution)/shard_map/ppermute | solution.py:43
  62.9 1.7 %collective-permute-done.24 = bf16[8,4096]{1,0:T(8,128)(2,1)S(1)} collective-permute-done((bf16[8,4096]{1,0:T(8,128)(2,1)S(1)}, bf16[8,4096]{1,0:T(8,128)(2,1)S(1)}, u32[]{:S(2)}, u32[]{:S(2)}) %collective-permute-start.24) | collective-permute-done | bytes 65568 | tf_op jit(solution)/shard_map/ppermute | solution.py:43
  65.5 0.8 %copy.9 = bf16[32,32,32]{1,2,0:T(8,128)(2,1)} copy(bf16[32,32,32]{2,1,0:T(8,128)(2,1)S(1)} %reshape.24) | data formatting | bytes 131072 | tf_op jit(solution)/shard_map/reshape | solution.py:272
  (53 shorter events, 6.0 us)
Async XLA Ops:
  2.0 8.7 %collective-permute-start = (bf16[32,1024]{1,0:T(8,128)(2,1)S(1)}, bf16[32,1024]{1,0:T(8,128)(2,1)S(1)}, u32[]{:S(2)}, u32[]{:S(2)}) collective-permute-start(bf16[32,1024]{1,0:T(8,128)(2,1)S(1)} %reshape.21), channel_id=1, source_target_pairs={{0,1},{1,0},{2,3},{3,2},{4,5},{5,4},{6,7},{7,6},{8,9},{9,8},{10,11... | collective-permute-start | bytes 196616 | tf_op jit(solution)/shard_map/ppermute | solution.py:59
  5.4 7.9 %collective-permute-start.3 = (bf16[8,4096]{1,0:T(8,128)(2,1)S(1)}, bf16[8,4096]{1,0:T(8,128)(2,1)S(1)}, u32[]{:S(2)}, u32[]{:S(2)}) collective-permute-start(bf16[8,4096]{1,0:T(8,128)(2,1)S(1)} %bitcast.15), channel_id=1, source_target_pairs={{0,64},{8,200},{16,80},{24,216},{32,96},{40,232},{48,112},{56,248}... | collective-permute-start | bytes 196616 | tf_op jit(solution)/shard_map/ppermute | solution.py:43
  10.8 7.8 %collective-permute-start.1 = (bf16[64,1024]{1,0:T(8,128)(2,1)S(1)}, bf16[64,1024]{1,0:T(8,128)(2,1)S(1)}, u32[]{:S(2)}, u32[]{:S(2)}) collective-permute-start(bf16[64,1024]{1,0:T(8,128)(2,1)S(1)} %pad_maximum_fusion.2), channel_id=1, source_target_pairs={{0,2},{1,3},{2,0},{3,1},{4,6},{5,7},{6,4},{7,5},{8,14},{9,15},{10,... | collective-permute-start | bytes 393224 | tf_op jit(solution)/shard_map/ppermute | solution.py:55
  13.3 6.5 %collective-permute-start.4 = (bf16[16,4096]{1,0:T(8,128)(2,1)S(1)}, bf16[16,4096]{1,0:T(8,128)(2,1)S(1)}, u32[]{:S(2)}, u32[]{:S(2)}) collective-permute-start(bf16[16,4096]{1,0:T(8,128)(2,1)S(1)} %pad_maximum_fusion.3), channel_id=1, source_target_pairs={{0,192},{8,72},{16,208},{24,88},{32,224},{40,104},{48,240},{56,120... | collective-permute-start | bytes 393224 | tf_op jit(solution)/shard_map/ppermute | solution.py:43
  18.6 6.9 %collective-permute-start.2 = (bf16[128,1024]{1,0:T(8,128)(2,1)S(1)}, bf16[128,1024]{1,0:T(8,128)(2,1)S(1)}, u32[]{:S(2)}, u32[]{:S(2)}) collective-permute-start(bf16[128,1024]{1,0:T(8,128)(2,1)S(1)} %pad_maximum_fusion.x0), channel_id=1, source_target_pairs={{0,6},{1,7},{2,4},{3,5},{4,2},{5,3},{6,0},{7,1},{8,10},{9,11},{10,... | collective-permute-start | bytes 786440 | tf_op jit(solution)/shard_map/ppermute | solution.py:55
  19.9 14.5 %collective-permute-start.6 = (bf16[32,4096]{1,0:T(8,128)(2,1)S(1)}, bf16[32,4096]{1,0:T(8,128)(2,1)S(1)}, u32[]{:S(2)}, u32[]{:S(2)}) collective-permute-start(bf16[32,4096]{1,0:T(8,128)(2,1)S(1)} %pad_maximum_fusion.1.b0), channel_id=1, source_target_pairs={{0,32},{8,40},{16,48},{24,56},{32,0},{40,8},{48,16},{56,24},{64,96... | collective-permute-start | bytes 786440 | tf_op jit(solution)/shard_map/ppermute | solution.py:47
  22.9 11.9 %collective-permute-start.7 = (bf16[32,4096]{1,0:T(8,128)(2,1)S(1)}, bf16[32,4096]{1,0:T(8,128)(2,1)S(1)}, u32[]{:S(2)}, u32[]{:S(2)}) collective-permute-start(bf16[32,4096]{1,0:T(8,128)(2,1)S(1)} %pad_maximum_fusion.1.b0), channel_id=1, source_target_pairs={{0,16},{8,24},{16,32},{24,40},{32,48},{40,56},{48,0},{56,8},{64,80... | collective-permute-start | bytes 786440 | tf_op jit(solution)/shard_map/ppermute | solution.py:47
  23.3 12.5 %collective-permute-start.5 = (bf16[32,4096]{1,0:T(8,128)(2,1)S(1)}, bf16[32,4096]{1,0:T(8,128)(2,1)S(1)}, u32[]{:S(2)}, u32[]{:S(2)}) collective-permute-start(bf16[32,4096]{1,0:T(8,128)(2,1)S(1)} %pad_maximum_fusion.1.b0), channel_id=1, source_target_pairs={{0,48},{8,56},{16,0},{24,8},{32,16},{40,24},{48,32},{56,40},{64,11... | collective-permute-start | bytes 786440 | tf_op jit(solution)/shard_map/ppermute | solution.py:47
  28.7 7.5 %collective-permute-start.16 = (bf16[32,4096]{1,0:T(8,128)(2,1)S(1)}, bf16[32,4096]{1,0:T(8,128)(2,1)S(1)}, u32[]{:S(2)}, u32[]{:S(2)}) collective-permute-start(bf16[32,4096]{1,0:T(8,128)(2,1)S(1)} %get-tuple-element.34), channel_id=1, source_target_pairs={{0,8},{8,0},{16,24},{24,16},{32,40},{40,32},{48,56},{56,48},{64,72... | collective-permute-start | bytes 786440 | tf_op jit(solution)/shard_map/ppermute | solution.py:51
  34.4 2.3 %collective-permute-start.20 = (bf16[32,4096]{1,0:T(8,128)(2,1)S(1)}, bf16[32,4096]{1,0:T(8,128)(2,1)S(1)}, u32[]{:S(2)}, u32[]{:S(2)}) collective-permute-start(bf16[32,4096]{1,0:T(8,128)(2,1)S(1)} %get-tuple-element.32), channel_id=1, source_target_pairs={{0,8},{8,0},{16,24},{24,16},{32,40},{40,32},{48,56},{56,48},{64,72... | collective-permute-start | bytes 786440 | tf_op jit(solution)/shard_map/ppermute | solution.py:51
  34.8 2.2 %collective-permute-start.8 = (bf16[32,4096]{1,0:T(8,128)(2,1)S(1)}, bf16[32,4096]{1,0:T(8,128)(2,1)S(1)}, u32[]{:S(2)}, u32[]{:S(2)}) collective-permute-start(bf16[32,4096]{1,0:T(8,128)(2,1)S(1)} %pad_maximum_fusion.1.b0), channel_id=1, source_target_pairs={{0,8},{8,0},{16,24},{24,16},{32,40},{40,32},{48,56},{56,48},{64,72... | collective-permute-start | bytes 786440 | tf_op jit(solution)/shard_map/ppermute | solution.py:51
  35.8 17.2 %collective-permute-start.15 = (bf16[32,4096]{1,0:T(8,128)(2,1)S(1)}, bf16[32,4096]{1,0:T(8,128)(2,1)S(1)}, u32[]{:S(2)}, u32[]{:S(2)}) collective-permute-start(bf16[32,4096]{1,0:T(8,128)(2,1)S(1)} %get-tuple-element.31), channel_id=1, source_target_pairs={{0,8},{8,0},{16,24},{24,16},{32,40},{40,32},{48,56},{56,48},{64,72... | collective-permute-start | bytes 786440 | tf_op jit(solution)/shard_map/ppermute | solution.py:51
  36.2 3.1 %collective-permute-start.10 = (bf16[32,4096]{1,0:T(8,128)(2,1)S(1)}, bf16[32,4096]{1,0:T(8,128)(2,1)S(1)}, u32[]{:S(2)}, u32[]{:S(2)}) collective-permute-start(bf16[32,4096]{1,0:T(8,128)(2,1)S(1)} %collective-permute-done.6.b2), channel_id=1, source_target_pairs={{0,8},{8,0},{16,24},{24,16},{32,40},{40,32},{48,56},{56,48},{64,72... | collective-permute-start | bytes 786440 | tf_op jit(solution)/shard_map/ppermute | solution.py:51
  36.3 3.7 %collective-permute-start.11 = (bf16[32,4096]{1,0:T(8,128)(2,1)S(1)}, bf16[32,4096]{1,0:T(8,128)(2,1)S(1)}, u32[]{:S(2)}, u32[]{:S(2)}) collective-permute-start(bf16[32,4096]{1,0:T(8,128)(2,1)S(1)} %collective-permute-done.7.b3), channel_id=1, source_target_pairs={{0,8},{8,0},{16,24},{24,16},{32,40},{40,32},{48,56},{56,48},{64,72... | collective-permute-start | bytes 786440 | tf_op jit(solution)/shard_map/ppermute | solution.py:51
  36.7 5.3 %collective-permute-start.9 = (bf16[32,4096]{1,0:T(8,128)(2,1)S(1)}, bf16[32,4096]{1,0:T(8,128)(2,1)S(1)}, u32[]{:S(2)}, u32[]{:S(2)}) collective-permute-start(bf16[32,4096]{1,0:T(8,128)(2,1)S(1)} %collective-permute-done.5.b1), channel_id=1, source_target_pairs={{0,8},{8,0},{16,24},{24,16},{32,40},{40,32},{48,56},{56,48},{64,72... | collective-permute-start | bytes 786440 | tf_op jit(solution)/shard_map/ppermute | solution.py:51
  37.1 16.0 %collective-permute-start.17 = (bf16[32,4096]{1,0:T(8,128)(2,1)S(1)}, bf16[32,4096]{1,0:T(8,128)(2,1)S(1)}, u32[]{:S(2)}, u32[]{:S(2)}) collective-permute-start(bf16[32,4096]{1,0:T(8,128)(2,1)S(1)} %get-tuple-element.28), channel_id=1, source_target_pairs={{0,32},{8,40},{16,48},{24,56},{32,0},{40,8},{48,16},{56,24},{64,96... | collective-permute-start | bytes 786440 | tf_op jit(solution)/shard_map/ppermute | solution.py:47
  39.3 13.8 %collective-permute-start.19 = (bf16[32,4096]{1,0:T(8,128)(2,1)S(1)}, bf16[32,4096]{1,0:T(8,128)(2,1)S(1)}, u32[]{:S(2)}, u32[]{:S(2)}) collective-permute-start(bf16[32,4096]{1,0:T(8,128)(2,1)S(1)} %get-tuple-element.30), channel_id=1, source_target_pairs={{0,16},{8,24},{16,32},{24,40},{32,48},{40,56},{48,0},{56,8},{64,80... | collective-permute-start | bytes 786440 | tf_op jit(solution)/shard_map/ppermute | solution.py:47
  40.0 13.0 %collective-permute-start.21 = (bf16[32,4096]{1,0:T(8,128)(2,1)S(1)}, bf16[32,4096]{1,0:T(8,128)(2,1)S(1)}, u32[]{:S(2)}, u32[]{:S(2)}) collective-permute-start(bf16[32,4096]{1,0:T(8,128)(2,1)S(1)} %get-tuple-element.29), channel_id=1, source_target_pairs={{0,48},{8,56},{16,0},{24,8},{32,16},{40,24},{48,32},{56,40},{64,11... | collective-permute-start | bytes 786440 | tf_op jit(solution)/shard_map/ppermute | solution.py:47
  44.9 5.9 %collective-permute-start.12 = (bf16[128,1024]{1,0:T(8,128)(2,1)S(1)}, bf16[128,1024]{1,0:T(8,128)(2,1)S(1)}, u32[]{:S(2)}, u32[]{:S(2)}) collective-permute-start(bf16[128,1024]{1,0:T(8,128)(2,1)S(1)} %get-tuple-element.20), channel_id=1, source_target_pairs={{0,6},{1,7},{2,4},{3,5},{4,2},{5,3},{6,0},{7,1},{8,10},{9,11},{10,... | collective-permute-start | bytes 786440 | tf_op jit(solution)/shard_map/ppermute | solution.py:55
  50.9 8.1 %collective-permute-start.13 = (bf16[64,1024]{1,0:T(8,128)(2,1)S(1)}, bf16[64,1024]{1,0:T(8,128)(2,1)S(1)}, u32[]{:S(2)}, u32[]{:S(2)}) collective-permute-start(bf16[64,1024]{1,0:T(8,128)(2,1)S(1)} %slice.100), channel_id=1, source_target_pairs={{0,2},{1,3},{2,0},{3,1},{4,6},{5,7},{6,4},{7,5},{8,14},{9,15},{10,... | collective-permute-start | bytes 393224 | tf_op jit(solution)/shard_map/ppermute | solution.py:55
  53.2 7.2 %collective-permute-start.22 = (bf16[8,4096]{1,0:T(8,128)(2,1)S(1)}, bf16[8,4096]{1,0:T(8,128)(2,1)S(1)}, u32[]{:S(2)}, u32[]{:S(2)}) collective-permute-start(bf16[8,4096]{1,0:T(8,128)(2,1)S(1)} %get-tuple-element.35), channel_id=1, source_target_pairs={{0,128},{8,136},{16,144},{24,152},{32,160},{40,168},{48,176},{56,1... | collective-permute-start | bytes 196616 | tf_op jit(solution)/shard_map/ppermute | solution.py:43
  57.5 5.3 %collective-permute-start.23 = (bf16[8,4096]{1,0:T(8,128)(2,1)S(1)}, bf16[8,4096]{1,0:T(8,128)(2,1)S(1)}, u32[]{:S(2)}, u32[]{:S(2)}) collective-permute-start(bf16[8,4096]{1,0:T(8,128)(2,1)S(1)} %get-tuple-element.37), channel_id=1, source_target_pairs={{0,64},{8,200},{16,80},{24,216},{32,96},{40,232},{48,112},{56,248}... | collective-permute-start | bytes 196616 | tf_op jit(solution)/shard_map/ppermute | solution.py:43
  57.5 7.1 %collective-permute-start.24 = (bf16[8,4096]{1,0:T(8,128)(2,1)S(1)}, bf16[8,4096]{1,0:T(8,128)(2,1)S(1)}, u32[]{:S(2)}, u32[]{:S(2)}) collective-permute-start(bf16[8,4096]{1,0:T(8,128)(2,1)S(1)} %get-tuple-element.36), channel_id=1, source_target_pairs={{0,192},{8,72},{16,208},{24,88},{32,224},{40,104},{48,240},{56,120... | collective-permute-start | bytes 196616 | tf_op jit(solution)/shard_map/ppermute | solution.py:43
  59.0 6.3 %collective-permute-start.14 = (bf16[32,1024]{1,0:T(8,128)(2,1)S(1)}, bf16[32,1024]{1,0:T(8,128)(2,1)S(1)}, u32[]{:S(2)}, u32[]{:S(2)}) collective-permute-start(bf16[32,1024]{1,0:T(8,128)(2,1)S(1)} %slice.101), channel_id=1, source_target_pairs={{0,1},{1,0},{2,3},{3,2},{4,5},{5,4},{6,7},{7,6},{8,9},{9,8},{10,11... | collective-permute-start | bytes 196616 | tf_op jit(solution)/shard_map/ppermute | solution.py:59
  (2 other events, 7.7 us)

commit v4 on v3

--- a/solution.py
+++ b/solution.py
@@ -261,7 +261,7 @@
     for k in (2, 1, 3):
         total = total + send_y(parts[k].astype(BF16), k).astype(F32)
     b_summed = total[:8]
-    for q, d in ((3, (2, 2)), (1, FIRST), (2, SECOND)):
+    for q, d in ((3, (2, 2)), (2, SECOND), (1, FIRST)):
         b_summed = b_summed + swap_z(total[8 * q:8 * (q + 1)].astype(BF16), d).astype(F32)
     grad_b = (b_summed * SCALE).astype(BF16).reshape(8, C, COLS)
 

time: 67.7 us -> 67.5 us (level); the launches traced: 66.4 us -> 67.3 us
  waiting for transfers between devices: 5.08 us -> 6.05 us
    ppermute x5, waiting for transfers between devices: 5.03 us -> 5.93 us  [swap_z(): return lax.ppermute(v, 'wide', wide_perm(d, 0, 0))]
  transfers between devices with their start and end apart: 25 -> 25, of which waited for: 3 -> 3; matrix products, arithmetic and copies ran while one was open for 3% -> 3% of each run, Pallas kernels for 23% -> 22%
where the time goes in v4:
time: 67.5 us; the launch traced here: 67.3 us
  starting transfers between devices  40.8 us (60%)
  Pallas kernels  15 us (22%)
  waiting for transfers between devices  6.05 us (9%)
  local copies, waits for them, and re-layouts  4.14 us (6%)
  between operations  0.8 us (1%)
    ppermute x5, starting transfers between devices, swap_z(): return lax.ppermute(v, 'wide', wide_perm(d, 0, 0))  12.2 us
    ppermute x6, starting transfers between devices, send_y(): return lax.ppermute(v, 'wide', wide_perm((0, 0), k, 0))  10.6 us
    ppermute x8, starting transfers between devices, swap_core(): return lax.ppermute(v, 'wide', wide_perm((0, 0), 0, 1))  8.16 us
    ppermute x4, starting transfers between devices, swap_x(): return lax.ppermute(v, ('wide', 'narrow'), x_perm(d))  6.72 us
    ppermute x5, waiting for transfers between devices, swap_z(): return lax.ppermute(v, 'wide', wide_perm(d, 0, 0))  5.93 us
    pallas_call x1, Pallas kernels, pair_update(): pl.pallas_call(update_kernel, grid=(ROWS // step,), in_specs=[pl.BlockSpe...  5.06 us
    pallas_call x1, Pallas kernels, grad_outer(): pl.pallas_call(grad_outer_kernel, grid=(ROWS // step,), in_specs=[pl.Bloc...  3.97 us
    ppermute x2, starting transfers between devices, swap_l(): return lax.ppermute(v, 'narrow', narrow_perm(1))  3.11 us
  transfers between devices with their start and end apart: 25, of which 3 were waited for; matrix products, arithmetic and copies ran while one was open for 3% of the time, Pallas kernels for 22%

profile of v4, /device:TPU:1, one launch (start us, length us, event | category | flops | bytes accessed | tf_op | source)
XLA Modules:
  0.0 67.3 jit_solution(9284509020074193963)
XLA Ops:
  0.6 1.1 %copy.8 = bf16[32,32,32]{2,1,0:T(8,128)(2,1)S(1)} copy(bf16[32,32,32]{1,2,0:T(8,128)(2,1)} %bitcast.18) | data formatting | bytes 131072 | tf_op jit(solution)/shard_map/transpose | solution.py:243
  2.0 2.6 %collective-permute-start = (bf16[32,1024]{1,0:T(8,128)(2,1)S(1)}, bf16[32,1024]{1,0:T(8,128)(2,1)S(1)}, u32[]{:S(2)}, u32[]{:S(2)}) collective-permute-start(bf16[32,1024]{1,0:T(8,128)(2,1)S(1)} %reshape.21), channel_id=1, source_target_pairs={{0,1},{1,0},{2,3},{3,2},{4,5},{5,4},{6,7},{7,6},{8,9},{9,8},{10,11... | collective-permute-start | bytes 196616 | tf_op jit(solution)/shard_map/ppermute | solution.py:59
  4.6 0.9 %copy.13 = bf16[1,8,32,128]{3,1,2,0:T(8,128)(2,1)S(1)} copy(bf16[1,8,32,128]{3,2,1,0:T(8,128)(2,1)} %bitcast.20) | data formatting | bytes 131072
  5.4 5.2 %collective-permute-start.3 = (bf16[8,4096]{1,0:T(8,128)(2,1)S(1)}, bf16[8,4096]{1,0:T(8,128)(2,1)S(1)}, u32[]{:S(2)}, u32[]{:S(2)}) collective-permute-start(bf16[8,4096]{1,0:T(8,128)(2,1)S(1)} %bitcast.15), channel_id=1, source_target_pairs={{0,64},{8,200},{16,80},{24,216},{32,96},{40,232},{48,112},{56,248}... | collective-permute-start | bytes 196616 | tf_op jit(solution)/shard_map/ppermute | solution.py:43
  10.8 2.6 %collective-permute-start.1 = (bf16[64,1024]{1,0:T(8,128)(2,1)S(1)}, bf16[64,1024]{1,0:T(8,128)(2,1)S(1)}, u32[]{:S(2)}, u32[]{:S(2)}) collective-permute-start(bf16[64,1024]{1,0:T(8,128)(2,1)S(1)} %pad_maximum_fusion.2), channel_id=1, source_target_pairs={{0,2},{1,3},{2,0},{3,1},{4,6},{5,7},{6,4},{7,5},{8,14},{9,15},{10,... | collective-permute-start | bytes 393224 | tf_op jit(solution)/shard_map/ppermute | solution.py:55
  13.3 1.3 %collective-permute-start.4 = (bf16[16,4096]{1,0:T(8,128)(2,1)S(1)}, bf16[16,4096]{1,0:T(8,128)(2,1)S(1)}, u32[]{:S(2)}, u32[]{:S(2)}) collective-permute-start(bf16[16,4096]{1,0:T(8,128)(2,1)S(1)} %pad_maximum_fusion.3), channel_id=1, source_target_pairs={{0,192},{8,72},{16,208},{24,88},{32,224},{40,104},{48,240},{56,120... | collective-permute-start | bytes 393224 | tf_op jit(solution)/shard_map/ppermute | solution.py:43
  14.6 4.0 %grad_outer.1 = (bf16[1024,4096]{1,0:T(8,128)(2,1)S(1)}, bf16[128,1024]{1,0:T(8,128)(2,1)S(1)}) custom-call(bf16[32,128,128]{2,1,0:T(8,128)(2,1)} %cot, bf16[1024,128]{1,0:T(8,128)(2,1)} %w.1), custom_call_target="tpu_custom_call" | custom-call | flops 1073741824 | bytes 9437184 | tf_op jit(solution)/shard_map/grad_outer/pallas_call | solution.py:96
  18.6 1.2 %collective-permute-start.2 = (bf16[128,1024]{1,0:T(8,128)(2,1)S(1)}, bf16[128,1024]{1,0:T(8,128)(2,1)S(1)}, u32[]{:S(2)}, u32[]{:S(2)}) collective-permute-start(bf16[128,1024]{1,0:T(8,128)(2,1)S(1)} %pad_maximum_fusion.x0), channel_id=1, source_target_pairs={{0,6},{1,7},{2,4},{3,5},{4,2},{5,3},{6,0},{7,1},{8,10},{9,11},{10,... | collective-permute-start | bytes 786440 | tf_op jit(solution)/shard_map/ppermute | solution.py:55
  19.9 3.0 %collective-permute-start.6 = (bf16[32,4096]{1,0:T(8,128)(2,1)S(1)}, bf16[32,4096]{1,0:T(8,128)(2,1)S(1)}, u32[]{:S(2)}, u32[]{:S(2)}) collective-permute-start(bf16[32,4096]{1,0:T(8,128)(2,1)S(1)} %pad_maximum_fusion.1.b0), channel_id=1, source_target_pairs={{0,32},{8,40},{16,48},{24,56},{32,0},{40,8},{48,16},{56,24},{64,96... | collective-permute-start | bytes 786440 | tf_op jit(solution)/shard_map/ppermute | solution.py:47
  23.3 2.3 %collective-permute-start.5 = (bf16[32,4096]{1,0:T(8,128)(2,1)S(1)}, bf16[32,4096]{1,0:T(8,128)(2,1)S(1)}, u32[]{:S(2)}, u32[]{:S(2)}) collective-permute-start(bf16[32,4096]{1,0:T(8,128)(2,1)S(1)} %pad_maximum_fusion.1.b0), channel_id=1, source_target_pairs={{0,48},{8,56},{16,0},{24,8},{32,16},{40,24},{48,32},{56,40},{64,11... | collective-permute-start | bytes 786440 | tf_op jit(solution)/shard_map/ppermute | solution.py:47
  25.6 3.0 %grad_b_terms.1 = (f32[128,4096]{1,0:T(8,128)S(1)}, bf16[128,4096]{1,0:T(8,128)(2,1)S(1)}, bf16[1024,256]{1,0:T(8,128)(2,1)S(1)}) custom-call(s32[5]{0:T(128)S(1)} %stack.23.place, bf16[128,1024]{1,0:T(8,128)(2,1)S(1)} %pad_maximum_fusion.x0, bf16[128,1024]{1,0:T(8,128)(2,1)S(1)} %collective-permute-done.2.x1, bf16[1024,4096]{1,0:T(8,128)(2,1)S(1)} %get-tuple-element.15.g), custom_call_target="tpu_custom_call" | custom-call | flops 2147483648 | bytes 12582912 | tf_op jit(solution)/shard_map/grad_b_terms/pallas_call | solution.py:146
  28.7 5.6 %collective-permute-start.16 = (bf16[32,4096]{1,0:T(8,128)(2,1)S(1)}, bf16[32,4096]{1,0:T(8,128)(2,1)S(1)}, u32[]{:S(2)}, u32[]{:S(2)}) collective-permute-start(bf16[32,4096]{1,0:T(8,128)(2,1)S(1)} %get-tuple-element.34), channel_id=1, source_target_pairs={{0,8},{8,0},{16,24},{24,16},{32,40},{40,32},{48,56},{56,48},{64,72... | collective-permute-start | bytes 786440 | tf_op jit(solution)/shard_map/ppermute | solution.py:51
  34.8 1.0 %collective-permute-start.8 = (bf16[32,4096]{1,0:T(8,128)(2,1)S(1)}, bf16[32,4096]{1,0:T(8,128)(2,1)S(1)}, u32[]{:S(2)}, u32[]{:S(2)}) collective-permute-start(bf16[32,4096]{1,0:T(8,128)(2,1)S(1)} %pad_maximum_fusion.1.b0), channel_id=1, source_target_pairs={{0,8},{8,0},{16,24},{24,16},{32,40},{40,32},{48,56},{56,48},{64,72... | collective-permute-start | bytes 786440 | tf_op jit(solution)/shard_map/ppermute | solution.py:51
  37.1 2.2 %collective-permute-start.17 = (bf16[32,4096]{1,0:T(8,128)(2,1)S(1)}, bf16[32,4096]{1,0:T(8,128)(2,1)S(1)}, u32[]{:S(2)}, u32[]{:S(2)}) collective-permute-start(bf16[32,4096]{1,0:T(8,128)(2,1)S(1)} %get-tuple-element.28), channel_id=1, source_target_pairs={{0,32},{8,40},{16,48},{24,56},{32,0},{40,8},{48,16},{56,24},{64,96... | collective-permute-start | bytes 786440 | tf_op jit(solution)/shard_map/ppermute | solution.py:47
  40.0 1.9 %collective-permute-start.21 = (bf16[32,4096]{1,0:T(8,128)(2,1)S(1)}, bf16[32,4096]{1,0:T(8,128)(2,1)S(1)}, u32[]{:S(2)}, u32[]{:S(2)}) collective-permute-start(bf16[32,4096]{1,0:T(8,128)(2,1)S(1)} %get-tuple-element.29), channel_id=1, source_target_pairs={{0,48},{8,56},{16,0},{24,8},{32,16},{40,24},{48,32},{56,40},{64,11... | collective-permute-start | bytes 786440 | tf_op jit(solution)/shard_map/ppermute | solution.py:47
  42.0 3.0 %grad_a_terms.1 = (f32[128,1024]{1,0:T(8,128)S(1)}, bf16[128,1024]{1,0:T(8,128)(2,1)S(1)}, bf16[256,4096]{1,0:T(8,128)(2,1)S(1)}) custom-call(s32[5]{0:T(128)S(1)} %stack.23.place, bf16[32,4096]{1,0:T(8,128)(2,1)S(1)} %pad_maximum_fusion.1.b0, bf16[32,4096]{1,0:T(8,128)(2,1)S(1)} %collective-permute-done.5.b1, ...), custom_call_target="tpu_custom_call" | custom-call | flops 2147483648 | bytes 12582912 | tf_op jit(solution)/shard_map/grad_a_terms/pallas_call | solution.py:184
  44.9 0.8 %collective-permute-start.12 = (bf16[128,1024]{1,0:T(8,128)(2,1)S(1)}, bf16[128,1024]{1,0:T(8,128)(2,1)S(1)}, u32[]{:S(2)}, u32[]{:S(2)}) collective-permute-start(bf16[128,1024]{1,0:T(8,128)(2,1)S(1)} %get-tuple-element.20), channel_id=1, source_target_pairs={{0,6},{1,7},{2,4},{3,5},{4,2},{5,3},{6,0},{7,1},{8,10},{9,11},{10,... | collective-permute-start | bytes 786440 | tf_op jit(solution)/shard_map/ppermute | solution.py:55
  45.7 5.1 %pair_update.1 = bf16[32,128,128]{2,1,0:T(8,128)(2,1)} custom-call(bf16[1024,256]{1,0:T(8,128)(2,1)S(1)} %get-tuple-element.16.at, bf16[256,4096]{1,0:T(8,128)(2,1)S(1)} %get-tuple-element.17.b, bf16[128,1024]{1,0:T(8,128)(2,1)S(1)} %get-tuple-element.18.wt, f32[1,128]{1,0:T(1,128)S(1)} %bitcast.14), custom_call_target="tpu_custom_call" | custom-call | flops 3221225472 | bytes 4194304 | tf_op jit(solution)/shard_map/pair_update/pallas_call | solution.py:217
  50.9 2.1 %collective-permute-start.13 = (bf16[64,1024]{1,0:T(8,128)(2,1)S(1)}, bf16[64,1024]{1,0:T(8,128)(2,1)S(1)}, u32[]{:S(2)}, u32[]{:S(2)}) collective-permute-start(bf16[64,1024]{1,0:T(8,128)(2,1)S(1)} %slice.100), channel_id=1, source_target_pairs={{0,2},{1,3},{2,0},{3,1},{4,6},{5,7},{6,4},{7,5},{8,14},{9,15},{10,... | collective-permute-start | bytes 393224 | tf_op jit(solution)/shard_map/ppermute | solution.py:55
  53.2 4.3 %collective-permute-start.22 = (bf16[8,4096]{1,0:T(8,128)(2,1)S(1)}, bf16[8,4096]{1,0:T(8,128)(2,1)S(1)}, u32[]{:S(2)}, u32[]{:S(2)}) collective-permute-start(bf16[8,4096]{1,0:T(8,128)(2,1)S(1)} %get-tuple-element.35), channel_id=1, source_target_pairs={{0,128},{8,136},{16,144},{24,152},{32,160},{40,168},{48,176},{56,1... | collective-permute-start | bytes 196616 | tf_op jit(solution)/shard_map/ppermute | solution.py:43
  58.1 0.9 %collective-permute-start.24 = (bf16[8,4096]{1,0:T(8,128)(2,1)S(1)}, bf16[8,4096]{1,0:T(8,128)(2,1)S(1)}, u32[]{:S(2)}, u32[]{:S(2)}) collective-permute-start(bf16[8,4096]{1,0:T(8,128)(2,1)S(1)} %get-tuple-element.36), channel_id=1, source_target_pairs={{0,64},{8,200},{16,80},{24,216},{32,96},{40,232},{48,112},{56,248}... | collective-permute-start | bytes 196616 | tf_op jit(solution)/shard_map/ppermute | solution.py:43
  59.6 0.8 %collective-permute-done.22 = bf16[8,4096]{1,0:T(8,128)(2,1)S(1)} collective-permute-done((bf16[8,4096]{1,0:T(8,128)(2,1)S(1)}, bf16[8,4096]{1,0:T(8,128)(2,1)S(1)}, u32[]{:S(2)}, u32[]{:S(2)}) %collective-permute-start.22) | collective-permute-done | bytes 65568 | tf_op jit(solution)/shard_map/ppermute | solution.py:43
  60.4 5.1 %collective-permute-done.23 = bf16[8,4096]{1,0:T(8,128)(2,1)S(1)} collective-permute-done((bf16[8,4096]{1,0:T(8,128)(2,1)S(1)}, bf16[8,4096]{1,0:T(8,128)(2,1)S(1)}, u32[]{:S(2)}, u32[]{:S(2)}) %collective-permute-start.23) | collective-permute-done | bytes 65568 | tf_op jit(solution)/shard_map/ppermute | solution.py:43
  66.5 0.8 %copy.9 = bf16[32,32,32]{1,2,0:T(8,128)(2,1)} copy(bf16[32,32,32]{2,1,0:T(8,128)(2,1)S(1)} %reshape.24) | data formatting | bytes 131072 | tf_op jit(solution)/shard_map/reshape | solution.py:272
  (53 shorter events, 5.8 us)
Async XLA Ops:
  2.0 8.7 %collective-permute-start = (bf16[32,1024]{1,0:T(8,128)(2,1)S(1)}, bf16[32,1024]{1,0:T(8,128)(2,1)S(1)}, u32[]{:S(2)}, u32[]{:S(2)}) collective-permute-start(bf16[32,1024]{1,0:T(8,128)(2,1)S(1)} %reshape.21), channel_id=1, source_target_pairs={{0,1},{1,0},{2,3},{3,2},{4,5},{5,4},{6,7},{7,6},{8,9},{9,8},{10,11... | collective-permute-start | bytes 196616 | tf_op jit(solution)/shard_map/ppermute | solution.py:59
  5.4 7.9 %collective-permute-start.3 = (bf16[8,4096]{1,0:T(8,128)(2,1)S(1)}, bf16[8,4096]{1,0:T(8,128)(2,1)S(1)}, u32[]{:S(2)}, u32[]{:S(2)}) collective-permute-start(bf16[8,4096]{1,0:T(8,128)(2,1)S(1)} %bitcast.15), channel_id=1, source_target_pairs={{0,64},{8,200},{16,80},{24,216},{32,96},{40,232},{48,112},{56,248}... | collective-permute-start | bytes 196616 | tf_op jit(solution)/shard_map/ppermute | solution.py:43
  10.8 7.8 %collective-permute-start.1 = (bf16[64,1024]{1,0:T(8,128)(2,1)S(1)}, bf16[64,1024]{1,0:T(8,128)(2,1)S(1)}, u32[]{:S(2)}, u32[]{:S(2)}) collective-permute-start(bf16[64,1024]{1,0:T(8,128)(2,1)S(1)} %pad_maximum_fusion.2), channel_id=1, source_target_pairs={{0,2},{1,3},{2,0},{3,1},{4,6},{5,7},{6,4},{7,5},{8,14},{9,15},{10,... | collective-permute-start | bytes 393224 | tf_op jit(solution)/shard_map/ppermute | solution.py:55
  13.3 6.5 %collective-permute-start.4 = (bf16[16,4096]{1,0:T(8,128)(2,1)S(1)}, bf16[16,4096]{1,0:T(8,128)(2,1)S(1)}, u32[]{:S(2)}, u32[]{:S(2)}) collective-permute-start(bf16[16,4096]{1,0:T(8,128)(2,1)S(1)} %pad_maximum_fusion.3), channel_id=1, source_target_pairs={{0,192},{8,72},{16,208},{24,88},{32,224},{40,104},{48,240},{56,120... | collective-permute-start | bytes 393224 | tf_op jit(solution)/shard_map/ppermute | solution.py:43
  18.6 6.9 %collective-permute-start.2 = (bf16[128,1024]{1,0:T(8,128)(2,1)S(1)}, bf16[128,1024]{1,0:T(8,128)(2,1)S(1)}, u32[]{:S(2)}, u32[]{:S(2)}) collective-permute-start(bf16[128,1024]{1,0:T(8,128)(2,1)S(1)} %pad_maximum_fusion.x0), channel_id=1, source_target_pairs={{0,6},{1,7},{2,4},{3,5},{4,2},{5,3},{6,0},{7,1},{8,10},{9,11},{10,... | collective-permute-start | bytes 786440 | tf_op jit(solution)/shard_map/ppermute | solution.py:55
  19.9 14.5 %collective-permute-start.6 = (bf16[32,4096]{1,0:T(8,128)(2,1)S(1)}, bf16[32,4096]{1,0:T(8,128)(2,1)S(1)}, u32[]{:S(2)}, u32[]{:S(2)}) collective-permute-start(bf16[32,4096]{1,0:T(8,128)(2,1)S(1)} %pad_maximum_fusion.1.b0), channel_id=1, source_target_pairs={{0,32},{8,40},{16,48},{24,56},{32,0},{40,8},{48,16},{56,24},{64,96... | collective-permute-start | bytes 786440 | tf_op jit(solution)/shard_map/ppermute | solution.py:47
  22.9 11.9 %collective-permute-start.7 = (bf16[32,4096]{1,0:T(8,128)(2,1)S(1)}, bf16[32,4096]{1,0:T(8,128)(2,1)S(1)}, u32[]{:S(2)}, u32[]{:S(2)}) collective-permute-start(bf16[32,4096]{1,0:T(8,128)(2,1)S(1)} %pad_maximum_fusion.1.b0), channel_id=1, source_target_pairs={{0,16},{8,24},{16,32},{24,40},{32,48},{40,56},{48,0},{56,8},{64,80... | collective-permute-start | bytes 786440 | tf_op jit(solution)/shard_map/ppermute | solution.py:47
  23.3 12.5 %collective-permute-start.5 = (bf16[32,4096]{1,0:T(8,128)(2,1)S(1)}, bf16[32,4096]{1,0:T(8,128)(2,1)S(1)}, u32[]{:S(2)}, u32[]{:S(2)}) collective-permute-start(bf16[32,4096]{1,0:T(8,128)(2,1)S(1)} %pad_maximum_fusion.1.b0), channel_id=1, source_target_pairs={{0,48},{8,56},{16,0},{24,8},{32,16},{40,24},{48,32},{56,40},{64,11... | collective-permute-start | bytes 786440 | tf_op jit(solution)/shard_map/ppermute | solution.py:47
  28.7 7.5 %collective-permute-start.16 = (bf16[32,4096]{1,0:T(8,128)(2,1)S(1)}, bf16[32,4096]{1,0:T(8,128)(2,1)S(1)}, u32[]{:S(2)}, u32[]{:S(2)}) collective-permute-start(bf16[32,4096]{1,0:T(8,128)(2,1)S(1)} %get-tuple-element.34), channel_id=1, source_target_pairs={{0,8},{8,0},{16,24},{24,16},{32,40},{40,32},{48,56},{56,48},{64,72... | collective-permute-start | bytes 786440 | tf_op jit(solution)/shard_map/ppermute | solution.py:51
  34.4 2.3 %collective-permute-start.20 = (bf16[32,4096]{1,0:T(8,128)(2,1)S(1)}, bf16[32,4096]{1,0:T(8,128)(2,1)S(1)}, u32[]{:S(2)}, u32[]{:S(2)}) collective-permute-start(bf16[32,4096]{1,0:T(8,128)(2,1)S(1)} %get-tuple-element.32), channel_id=1, source_target_pairs={{0,8},{8,0},{16,24},{24,16},{32,40},{40,32},{48,56},{56,48},{64,72... | collective-permute-start | bytes 786440 | tf_op jit(solution)/shard_map/ppermute | solution.py:51
  34.8 2.2 %collective-permute-start.8 = (bf16[32,4096]{1,0:T(8,128)(2,1)S(1)}, bf16[32,4096]{1,0:T(8,128)(2,1)S(1)}, u32[]{:S(2)}, u32[]{:S(2)}) collective-permute-start(bf16[32,4096]{1,0:T(8,128)(2,1)S(1)} %pad_maximum_fusion.1.b0), channel_id=1, source_target_pairs={{0,8},{8,0},{16,24},{24,16},{32,40},{40,32},{48,56},{56,48},{64,72... | collective-permute-start | bytes 786440 | tf_op jit(solution)/shard_map/ppermute | solution.py:51
  35.8 17.2 %collective-permute-start.15 = (bf16[32,4096]{1,0:T(8,128)(2,1)S(1)}, bf16[32,4096]{1,0:T(8,128)(2,1)S(1)}, u32[]{:S(2)}, u32[]{:S(2)}) collective-permute-start(bf16[32,4096]{1,0:T(8,128)(2,1)S(1)} %get-tuple-element.31), channel_id=1, source_target_pairs={{0,8},{8,0},{16,24},{24,16},{32,40},{40,32},{48,56},{56,48},{64,72... | collective-permute-start | bytes 786440 | tf_op jit(solution)/shard_map/ppermute | solution.py:51
  36.2 3.1 %collective-permute-start.10 = (bf16[32,4096]{1,0:T(8,128)(2,1)S(1)}, bf16[32,4096]{1,0:T(8,128)(2,1)S(1)}, u32[]{:S(2)}, u32[]{:S(2)}) collective-permute-start(bf16[32,4096]{1,0:T(8,128)(2,1)S(1)} %collective-permute-done.6.b2), channel_id=1, source_target_pairs={{0,8},{8,0},{16,24},{24,16},{32,40},{40,32},{48,56},{56,48},{64,72... | collective-permute-start | bytes 786440 | tf_op jit(solution)/shard_map/ppermute | solution.py:51
  36.3 3.7 %collective-permute-start.11 = (bf16[32,4096]{1,0:T(8,128)(2,1)S(1)}, bf16[32,4096]{1,0:T(8,128)(2,1)S(1)}, u32[]{:S(2)}, u32[]{:S(2)}) collective-permute-start(bf16[32,4096]{1,0:T(8,128)(2,1)S(1)} %collective-permute-done.7.b3), channel_id=1, source_target_pairs={{0,8},{8,0},{16,24},{24,16},{32,40},{40,32},{48,56},{56,48},{64,72... | collective-permute-start | bytes 786440 | tf_op jit(solution)/shard_map/ppermute | solution.py:51
  36.7 5.3 %collective-permute-start.9 = (bf16[32,4096]{1,0:T(8,128)(2,1)S(1)}, bf16[32,4096]{1,0:T(8,128)(2,1)S(1)}, u32[]{:S(2)}, u32[]{:S(2)}) collective-permute-start(bf16[32,4096]{1,0:T(8,128)(2,1)S(1)} %collective-permute-done.5.b1), channel_id=1, source_target_pairs={{0,8},{8,0},{16,24},{24,16},{32,40},{40,32},{48,56},{56,48},{64,72... | collective-permute-start | bytes 786440 | tf_op jit(solution)/shard_map/ppermute | solution.py:51
  37.1 16.0 %collective-permute-start.17 = (bf16[32,4096]{1,0:T(8,128)(2,1)S(1)}, bf16[32,4096]{1,0:T(8,128)(2,1)S(1)}, u32[]{:S(2)}, u32[]{:S(2)}) collective-permute-start(bf16[32,4096]{1,0:T(8,128)(2,1)S(1)} %get-tuple-element.28), channel_id=1, source_target_pairs={{0,32},{8,40},{16,48},{24,56},{32,0},{40,8},{48,16},{56,24},{64,96... | collective-permute-start | bytes 786440 | tf_op jit(solution)/shard_map/ppermute | solution.py:47
  39.3 13.8 %collective-permute-start.19 = (bf16[32,4096]{1,0:T(8,128)(2,1)S(1)}, bf16[32,4096]{1,0:T(8,128)(2,1)S(1)}, u32[]{:S(2)}, u32[]{:S(2)}) collective-permute-start(bf16[32,4096]{1,0:T(8,128)(2,1)S(1)} %get-tuple-element.30), channel_id=1, source_target_pairs={{0,16},{8,24},{16,32},{24,40},{32,48},{40,56},{48,0},{56,8},{64,80... | collective-permute-start | bytes 786440 | tf_op jit(solution)/shard_map/ppermute | solution.py:47
  40.0 13.0 %collective-permute-start.21 = (bf16[32,4096]{1,0:T(8,128)(2,1)S(1)}, bf16[32,4096]{1,0:T(8,128)(2,1)S(1)}, u32[]{:S(2)}, u32[]{:S(2)}) collective-permute-start(bf16[32,4096]{1,0:T(8,128)(2,1)S(1)} %get-tuple-element.29), channel_id=1, source_target_pairs={{0,48},{8,56},{16,0},{24,8},{32,16},{40,24},{48,32},{56,40},{64,11... | collective-permute-start | bytes 786440 | tf_op jit(solution)/shard_map/ppermute | solution.py:47
  44.9 5.9 %collective-permute-start.12 = (bf16[128,1024]{1,0:T(8,128)(2,1)S(1)}, bf16[128,1024]{1,0:T(8,128)(2,1)S(1)}, u32[]{:S(2)}, u32[]{:S(2)}) collective-permute-start(bf16[128,1024]{1,0:T(8,128)(2,1)S(1)} %get-tuple-element.20), channel_id=1, source_target_pairs={{0,6},{1,7},{2,4},{3,5},{4,2},{5,3},{6,0},{7,1},{8,10},{9,11},{10,... | collective-permute-start | bytes 786440 | tf_op jit(solution)/shard_map/ppermute | solution.py:55
  50.9 8.1 %collective-permute-start.13 = (bf16[64,1024]{1,0:T(8,128)(2,1)S(1)}, bf16[64,1024]{1,0:T(8,128)(2,1)S(1)}, u32[]{:S(2)}, u32[]{:S(2)}) collective-permute-start(bf16[64,1024]{1,0:T(8,128)(2,1)S(1)} %slice.100), channel_id=1, source_target_pairs={{0,2},{1,3},{2,0},{3,1},{4,6},{5,7},{6,4},{7,5},{8,14},{9,15},{10,... | collective-permute-start | bytes 393224 | tf_op jit(solution)/shard_map/ppermute | solution.py:55
  53.2 7.2 %collective-permute-start.22 = (bf16[8,4096]{1,0:T(8,128)(2,1)S(1)}, bf16[8,4096]{1,0:T(8,128)(2,1)S(1)}, u32[]{:S(2)}, u32[]{:S(2)}) collective-permute-start(bf16[8,4096]{1,0:T(8,128)(2,1)S(1)} %get-tuple-element.35), channel_id=1, source_target_pairs={{0,128},{8,136},{16,144},{24,152},{32,160},{40,168},{48,176},{56,1... | collective-permute-start | bytes 196616 | tf_op jit(solution)/shard_map/ppermute | solution.py:43
  57.5 8.0 %collective-permute-start.23 = (bf16[8,4096]{1,0:T(8,128)(2,1)S(1)}, bf16[8,4096]{1,0:T(8,128)(2,1)S(1)}, u32[]{:S(2)}, u32[]{:S(2)}) collective-permute-start(bf16[8,4096]{1,0:T(8,128)(2,1)S(1)} %get-tuple-element.37), channel_id=1, source_target_pairs={{0,192},{8,72},{16,208},{24,88},{32,224},{40,104},{48,240},{56,120... | collective-permute-start | bytes 196616 | tf_op jit(solution)/shard_map/ppermute | solution.py:43
  58.1 7.4 %collective-permute-start.24 = (bf16[8,4096]{1,0:T(8,128)(2,1)S(1)}, bf16[8,4096]{1,0:T(8,128)(2,1)S(1)}, u32[]{:S(2)}, u32[]{:S(2)}) collective-permute-start(bf16[8,4096]{1,0:T(8,128)(2,1)S(1)} %get-tuple-element.36), channel_id=1, source_target_pairs={{0,64},{8,200},{16,80},{24,216},{32,96},{40,232},{48,112},{56,248}... | collective-permute-start | bytes 196616 | tf_op jit(solution)/shard_map/ppermute | solution.py:43
  59.0 7.2 %collective-permute-start.14 = (bf16[32,1024]{1,0:T(8,128)(2,1)S(1)}, bf16[32,1024]{1,0:T(8,128)(2,1)S(1)}, u32[]{:S(2)}, u32[]{:S(2)}) collective-permute-start(bf16[32,1024]{1,0:T(8,128)(2,1)S(1)} %slice.101), channel_id=1, source_target_pairs={{0,1},{1,0},{2,3},{3,2},{4,5},{5,4},{6,7},{7,6},{8,9},{9,8},{10,11... | collective-permute-start | bytes 196616 | tf_op jit(solution)/shard_map/ppermute | solution.py:59
  (2 other events, 7.7 us)
